TPU v7x, 32 devices: a whole 2x2x4 slice. The times are simulated.
32 devices in a mesh: groups: 2 (over x), expert: 16 (over z, y, core).
Axes of the slice: x: 2, y: 2, z: 4, core: 2. Of those that a mesh axis runs over, the one named last changes fastest.
Arguments:
- tokens: bfloat16 [4096, 2048], P(('groups', 'expert')), parts along dimension 0, may hold values from -6 to 6
- grad_out: bfloat16 [4096, 2048], P(('groups', 'expert')), parts along dimension 0, may hold values from -6 to 6
- routes: int32 [4096, 8], P(('groups', 'expert')), parts along dimension 0, may hold values from 0 to 31, all different within a row; in each aligned block of 128 rows (0 to 127, 128 to 255, ...) at most 40 rows name the same one
- combine_weights: float32 [4096, 8], P(('groups', 'expert')), parts along dimension 0, may hold values from 0.05 to 0.5
- w_gate: bfloat16 [32, 2048, 768], P('expert'), may hold values from -0.125 to 0.125
- w_up: bfloat16 [32, 2048, 768], P('expert'), may hold values from -0.125 to 0.125
- w_down: bfloat16 [32, 768, 2048], P('expert'), may hold values from -0.21875 to 0.21875
Outputs:
- combined: bfloat16 [4096, 2048], P(('groups', 'expert')), parts along dimension 0
- grad_tokens: bfloat16 [4096, 2048], P(('groups', 'expert')), parts along dimension 0
- grad_weights: float32 [4096, 8], P(('groups', 'expert')), parts along dimension 0
There are 2 independent parts, one for each index of `groups`. A program takes and returns all parts, laid end to end along the dimension named above; an argument that names none is the same for every part. Nothing has to cross between parts.
Inputs may be any that keep to these rules, and one draw needn't show every extreme that they name: `routes`: each token names 8 different experts. Among the 128 tokens of one device (aligned blocks of rows) no expert is named more than 40 times.
All inputs are finite; a program needn't handle non-finite values.
Results may differ from a plain program's by a relative error of at most 0.0065.
Values may be sent and summed in bfloat16 or wider, within the bound.
A program may use at most 192 MiB of HBM per device.

v0:
```python
import jax
import jax.numpy as jnp
from jax import lax
from jax.sharding import PartitionSpec as P


def forward_part(rows_x, w_gate, w_up, w_down):
    gate_pre = jnp.einsum("necd,edf->necf", rows_x, w_gate, preferred_element_type=jnp.float32)
    up_pre = jnp.einsum("necd,edf->necf", rows_x, w_up, preferred_element_type=jnp.float32)
    squash = jax.nn.sigmoid(gate_pre)
    hidden = (gate_pre * squash * up_pre).astype(jnp.bfloat16)
    expert_out = jnp.einsum("necf,efd->necd", hidden, w_down, preferred_element_type=jnp.float32)
    return (expert_out.astype(jnp.bfloat16), gate_pre, up_pre)


def backward_part(rows_grad, gate_pre, up_pre, w_gate, w_up, w_down):
    squash = jax.nn.sigmoid(gate_pre)
    hidden_grad = jnp.einsum(
        "necd,efd->necf", rows_grad, w_down, preferred_element_type=jnp.float32
    )
    gate_grad = (hidden_grad * up_pre * squash * (1.0 + gate_pre * (1.0 - squash))).astype(
        jnp.bfloat16
    )
    up_grad = (hidden_grad * gate_pre * squash).astype(jnp.bfloat16)
    row_grad = jnp.einsum("necf,edf->necd", gate_grad, w_gate, preferred_element_type=jnp.float32)
    row_grad = row_grad + jnp.einsum(
        "necf,edf->necd", up_grad, w_up, preferred_element_type=jnp.float32
    )
    return row_grad.astype(jnp.bfloat16)


def shards(tokens, grad_out, routes, combine_weights, w_gate, w_up, w_down):
    node_count = lax.axis_size("expert")
    per_node = w_gate.shape[0]
    tok_rows, top_count = routes.shape
    model_width = tokens.shape[1]
    experts = per_node * node_count
    capacity = 5 * tok_rows * top_count // (4 * experts)
    matches = routes[:, :, None] == jnp.arange(experts, dtype=jnp.int32)[None, None, :]
    chosen = jnp.any(matches, axis=1).astype(jnp.int32)
    before = jnp.cumsum(chosen, axis=0, dtype=jnp.int32) - chosen
    position = jnp.sum(jnp.where(matches, before[:, None, :], 0), axis=2)
    slot_of = routes * capacity + position
    flat_slot = slot_of.reshape(-1)
    landing = jnp.arange(experts * capacity, dtype=jnp.int32)[:, None] == flat_slot[None, :]
    filled = jnp.any(landing, axis=1)
    row_ids = jnp.arange(flat_slot.shape[0], dtype=jnp.int32)
    owner_row = jnp.sum(jnp.where(landing, row_ids[None, :], 0), axis=1)
    slot_shape = (node_count, per_node, capacity, model_width)
    send_x = jnp.where(filled[:, None], tokens[owner_row // top_count], 0)
    send_x = send_x.reshape(slot_shape)
    grad_rows = (combine_weights[:, :, None] * grad_out[:, None, :].astype(jnp.float32)).astype(
        jnp.bfloat16
    )
    grad_rows = grad_rows.reshape(-1, model_width)
    send_grad = jnp.where(filled[:, None], grad_rows[owner_row], 0)
    send_grad = send_grad.reshape(slot_shape)
    arrived_x = lax.all_to_all(send_x, "expert", split_axis=0, concat_axis=0, tiled=True)
    expert_out, gate_pre, up_pre = forward_part(arrived_x, w_gate, w_up, w_down)
    back_out = lax.all_to_all(expert_out, "expert", split_axis=0, concat_axis=0, tiled=True)
    arrived_grad = lax.all_to_all(send_grad, "expert", split_axis=0, concat_axis=0, tiled=True)
    row_grad = backward_part(arrived_grad, gate_pre, up_pre, w_gate, w_up, w_down)
    back_grad = lax.all_to_all(row_grad, "expert", split_axis=0, concat_axis=0, tiled=True)
    out_rows = back_out.reshape(-1, model_width)[slot_of].astype(jnp.float32)
    grad_back = back_grad.reshape(-1, model_width)[slot_of].astype(jnp.float32)
    combined = jnp.sum(combine_weights[:, :, None] * out_rows, axis=1).astype(jnp.bfloat16)
    grad_weights = jnp.sum(grad_out.astype(jnp.float32)[:, None, :] * out_rows, axis=2)
    grad_tokens = jnp.sum(grad_back, axis=1).astype(jnp.bfloat16)
    return (combined, grad_tokens, grad_weights)


def solution(mesh):
    placed = (
        P(("groups", "expert"), None),
        P(("groups", "expert"), None),
        P(("groups", "expert"), None),
        P(("groups", "expert"), None),
        P("expert", None, None),
        P("expert", None, None),
        P("expert", None, None),
    )
    return jax.shard_map(
        shards,
        mesh=mesh,
        in_specs=placed,
        out_specs=(
            P(("groups", "expert"), None),
            P(("groups", "expert"), None),
            P(("groups", "expert"), None),
        ),
        check_vma=False,
    )
```

profile of v0, /device:TPU:13, one launch (start us, length us, event | category | flops | bytes accessed | tf_op | source)
XLA Modules:
  0.0 537.1 jit_solution(8485558343773565443)
XLA Ops:
  0.6 0.0 copy-start
  0.6 0.8 fusion.40
  1.4 0.1 copy.34
  1.6 0.2 reduce_window_sum.11
  1.7 0.1 copy.35
  1.8 0.7 select_reduce_fusion.1
  2.5 0.7 compare_select_fusion.1
  3.2 0.1 copy.36
  3.3 0.1 eq.32
  3.4 0.7 fusion.17
  4.1 0.6 select_reduce_fusion
  4.7 0.8 copy.33
  5.5 0.1 mul.68
  5.6 0.1 broadcast_in_dim.61
  5.7 0.1 fusion.41
  5.8 1.1 convert_element_type.58
  6.9 2.4 fusion.2
  9.3 13.6 %gather_fusion.2 = bf16[1280,2048]{1,0:T(8,128)(2,1)} fusion(bf16[1024,2048]{1,0:T(8,128)(2,1)} %fusion.2, s32[2048]{0:T(1024)S(1)} %get-tuple-element.17), kind=kCustom, calls=%fused_computation.2 | custom fusion | bytes 10490880 | tf_op jit(solution)/shard_map/gather | solution.py:56
  22.8 0.0 copy-done
  22.8 6.2 %gather_fusion = bf16[1280,2048]{1,0:T(8,128)(2,1)} fusion(bf16[128,2048]{1,0:T(8,128)(2,1)S(1)} %copy-done, s32[2048]{0:T(1024)S(1)} %get-tuple-element.18), kind=kCustom, calls=%fused_computation | custom fusion | bytes 10490880 | tf_op jit(solution)/shard_map/gather | solution.py:50
  29.0 8.8 %broadcast_select_fusion = (bf16[16,2,40,2048]{3,2,1,0:T(8,128)(2,1)}, bf16[16,2,40,2048]{3,2,1,0:T(8,128)(2,1)}) fusion(bf16[16,2,40,2048]{3,2,1,0:T(8,128)(2,1)} %bitcast.91, pred[16,2,40]{2,1,0:T(4,128)(4,1)S(1)} %broadcast_in_dim.61, bf16[16,2,40,2048]{3,2,1,0:T(8,128)(2,1)} %bitcast.92), kind=kLoop, calls=%fused_computation.29 | loop fusion | flops 5242880 | bytes 20972800 | tf_op jit(solution)/shard_map/jit(_where)/select_n | solution.py:56
  37.8 121.4 %all_to_all.20 = bf16[16,2,40,2048]{3,2,1,0:T(8,128)(2,1)} all-to-all(bf16[16,2,40,2048]{3,2,1,0:T(8,128)(2,1)} %get-tuple-element.16), channel_id=1, replica_groups=mesh['groups'=2,'expert'=16] {'expert'}, dimensions={0} | all-to-all | bytes 10485760 | tf_op jit(solution)/shard_map/all_to_all | solution.py:58
  159.2 5.4 %all-to-all-start.2 = ((bf16[16,2,40,2048]{3,2,1,0:T(8,128)(2,1)}), bf16[16,2,40,2048]{3,2,1,0:T(8,128)(2,1)}, u32[]{:S(2)}, u32[]{:S(2)}) async-start(bf16[16,2,40,2048]{3,2,1,0:T(8,128)(2,1)} %get-tuple-element.15), calls=%async_computation.2 | async-start | bytes 10485760 | tf_op jit(solution)/shard_map/all_to_all | solution.py:61
  164.6 0.0 copy-start.2
  164.6 8.2 %fusion.9 = f32[2,16,40,768]{3,2,1,0:T(8,128)S(1)} fusion(bf16[2,2048,768]{2,1,0:T(8,128)(2,1)} %param.11, bf16[16,2,40,2048]{3,2,1,0:T(8,128)(2,1)} %all_to_all.20), kind=kOutput, calls=%fused_computation.17 | convolution fusion | flops 4026531840 | bytes 15466496 | tf_op jit(solution)/shard_map/necd,edf->necf/dot_general | solution.py:8
  172.7 0.0 copy-done.2
  172.7 0.0 copy-start.3
  172.8 10.4 %fusion.5 = f32[2,16,40,768]{3,2,1,0:T(8,128)} fusion(bf16[2,2048,768]{2,1,0:T(8,128)(2,1)} %param.12, bf16[16,2,40,2048]{3,2,1,0:T(8,128)(2,1)S(1)} %copy-done.2), kind=kOutput, calls=%fused_computation.13 | convolution fusion | flops 4026531840 | bytes 15466496 | tf_op jit(solution)/shard_map/necd,edf->necf/dot_general | solution.py:9
  183.2 0.0 copy-done.3
  183.2 8.3 %convert_bitcast_fusion = bf16[16,2,40,2048]{3,2,0,1:T(8,128)(2,1)S(1)} fusion(bf16[2,768,2048]{2,1,0:T(8,128)(2,1)} %param.13, f32[2,16,40,768]{3,2,1,0:T(8,128)} %fusion.5, f32[2,16,40,768]{3,2,1,0:T(8,128)S(1)} %fusion.9), kind=kOutput, calls=%fused_computation.25 | convolution fusion | flops 4035051520 | bytes 19398656 | tf_op jit(solution)/shard_map/necf,efd->necd/dot_general | solution.py:12
  191.5 2.7 copy.39
  194.2 85.3 %all-to-all-done.2 = bf16[16,2,40,2048]{3,2,1,0:T(8,128)(2,1)} async-done(((bf16[16,2,40,2048]{3,2,1,0:T(8,128)(2,1)}), bf16[16,2,40,2048]{3,2,1,0:T(8,128)(2,1)}, u32[]{:S(2)}, u32[]{:S(2)}) %all-to-all-start.2) | async-done | bytes 5242912 | tf_op jit(solution)/shard_map/all_to_all | solution.py:61
  279.5 4.9 all-to-all-start.1
  284.4 0.0 copy-start.4
  284.4 10.7 %fusion.11 = f32[2,16,40,768]{3,2,1,0:T(8,128)} fusion(bf16[2,768,2048]{2,1,0:T(8,128)(2,1)} %param.13, bf16[16,2,40,2048]{3,2,1,0:T(8,128)(2,1)} %all-to-all-done.2), kind=kOutput, calls=%fused_computation.19 | convolution fusion | flops 4026531840 | bytes 15466496 | tf_op jit(solution)/shard_map/necd,efd->necf/dot_general | solution.py:18
  295.1 0.0 copy-done.4
  295.1 12.3 %fusion.3 = f32[2,16,40,2048]{3,2,1,0:T(8,128)} fusion(bf16[2,2048,768]{2,1,0:T(8,128)(2,1)} %param.12, f32[2,16,40,768]{3,2,1,0:T(8,128)} %fusion.11, f32[2,16,40,768]{3,2,1,0:T(8,128)S(1)} %copy-done.4), kind=kOutput, calls=%fused_computation.11 | convolution fusion | flops 4032430080 | bytes 24641536 | tf_op jit(solution)/shard_map/necf,edf->necd/dot_general | solution.py:26
  307.5 13.4 %fusion.15 = bf16[16,2,40,2048]{3,2,0,1:T(8,128)(2,1)} fusion(f32[2,16,40,2048]{3,2,1,0:T(8,128)} %fusion.3, bf16[2,2048,768]{2,1,0:T(8,128)(2,1)} %param.11, f32[2,16,40,768]{3,2,1,0:T(8,128)} %fusion.11, f32[2,16,40,768]{3,2,1,0:T(8,128)} %fusion.5, f32[2,16,40,768]{3,2,1,0:T(8,128)} %copy-done.3), kind=kOutput, calls=%fused_computation.23 | convolution fusion | flops 4041605120 | bytes 33816576 | tf_op jit(solution)/shard_map/necf,edf->necd/dot_general | solution.py:25
  320.9 5.7 %copy.43 = bf16[16,2,40,2048]{3,2,1,0:T(8,128)(2,1)} copy(bf16[16,2,40,2048]{3,2,0,1:T(8,128)(2,1)} %fusion.15) | data formatting | bytes 10485760 | tf_op jit(solution)/shard_map/convert_element_type | solution.py:29
  326.6 72.8 %all-to-all-done.1 = bf16[16,2,40,2048]{3,2,1,0:T(8,128)(2,1)} async-done(((bf16[16,2,40,2048]{3,2,1,0:T(8,128)(2,1)}), bf16[16,2,40,2048]{3,2,1,0:T(8,128)(2,1)}, u32[]{:S(2)}, u32[]{:S(2)}) %all-to-all-start.1) | async-done | bytes 5242912 | tf_op jit(solution)/shard_map/all_to_all | solution.py:60
  399.3 4.9 all-to-all-start.3
  404.2 0.1 copy.40
  404.4 0.1 reshape.127
  404.5 12.0 %gather_fusion.1 = bf16[1024,2048]{1,0:T(8,128)(2,1)} fusion(bf16[1280,2048]{1,0:T(8,128)(2,1)} %bitcast.10, s32[1024]{0:T(1024)S(1)} %broadcast_clamp_fusion), kind=kCustom, calls=%fused_computation.1 | custom fusion | bytes 8392704 | tf_op jit(solution)/shard_map/gather | solution.py:64
  416.5 5.7 %fusion.1 = (f32[128,8]{1,0:T(8,128)S(1)}, bf16[128,2048]{1,0:T(8,128)(2,1)}) fusion(bf16[1024,2048]{1,0:T(8,128)(2,1)} %gather_fusion.1, f32[128,2048]{1,0:T(8,128)S(1)} %convert_element_type.58, f32[128,8]{1,0:T(8,128)S(1)} %copy.33), kind=kLoop, calls=%fused_computation.8 | loop fusion | flops 10222592 | bytes 5775360 | tf_op jit(solution)/shard_map/reduce_sum | solution.py:67
  422.2 0.7 copy.44
  422.8 96.4 %all-to-all-done.3 = bf16[16,2,40,2048]{3,2,1,0:T(8,128)(2,1)} async-done(((bf16[16,2,40,2048]{3,2,1,0:T(8,128)(2,1)}), bf16[16,2,40,2048]{3,2,1,0:T(8,128)(2,1)}, u32[]{:S(2)}, u32[]{:S(2)}) %all-to-all-start.3) | async-done | bytes 5242912 | tf_op jit(solution)/shard_map/all_to_all | solution.py:63
  519.2 0.0 copy-start.1
  519.2 12.0 %gather_fusion.3 = bf16[1024,2048]{1,0:T(8,128)(2,1)} fusion(bf16[1280,2048]{1,0:T(8,128)(2,1)} %bitcast.19, s32[1024]{0:T(1024)S(1)} %broadcast_clamp_fusion), kind=kCustom, calls=%fused_computation.3 | custom fusion | bytes 8392704 | tf_op jit(solution)/shard_map/gather | solution.py:65
  531.2 5.9 %bitcast_reduce_fusion = bf16[128,2048]{1,0:T(8,128)(2,1)} fusion(bf16[1024,2048]{1,0:T(8,128)(2,1)} %gather_fusion.3), kind=kLoop, calls=%fused_computation.33 | loop fusion | flops 1835008 | bytes 4718592 | tf_op jit(solution)/shard_map/reduce_sum | solution.py:68
  537.1 0.0 copy-done.1
  (4 shorter events, 0.0 us)
Async XLA Ops:
  0.6 22.2 %copy-start = (bf16[128,2048]{1,0:T(8,128)(2,1)S(1)}, bf16[128,2048]{1,0:T(8,128)(2,1)}, u32[]{:S(2)}) copy-start(bf16[128,2048]{1,0:T(8,128)(2,1)} %param.7) | copy-start | bytes 1572868
  159.2 120.3 %all-to-all-start.2 = ((bf16[16,2,40,2048]{3,2,1,0:T(8,128)(2,1)}), bf16[16,2,40,2048]{3,2,1,0:T(8,128)(2,1)}, u32[]{:S(2)}, u32[]{:S(2)}) async-start(bf16[16,2,40,2048]{3,2,1,0:T(8,128)(2,1)} %get-tuple-element.15), calls=%async_computation.2 | async-start | bytes 10485760 | tf_op jit(solution)/shard_map/all_to_all | solution.py:61
  164.6 8.2 %copy-start.2 = (bf16[16,2,40,2048]{3,2,1,0:T(8,128)(2,1)S(1)}, bf16[16,2,40,2048]{3,2,1,0:T(8,128)(2,1)}, u32[]{:S(2)}) copy-start(bf16[16,2,40,2048]{3,2,1,0:T(8,128)(2,1)} %all_to_all.20) | copy-start | bytes 15728644
  172.7 10.4 %copy-start.3 = (f32[2,16,40,768]{3,2,1,0:T(8,128)}, f32[2,16,40,768]{3,2,1,0:T(8,128)S(1)}, u32[]{:S(2)}) copy-start(f32[2,16,40,768]{3,2,1,0:T(8,128)S(1)} %fusion.9) | copy-start | bytes 11796484
  279.5 119.8 %all-to-all-start.1 = ((bf16[16,2,40,2048]{3,2,1,0:T(8,128)(2,1)}), bf16[16,2,40,2048]{3,2,1,0:T(8,128)(2,1)}, u32[]{:S(2)}, u32[]{:S(2)}) async-start(bf16[16,2,40,2048]{3,2,1,0:T(8,128)(2,1)} %copy.39), calls=%async_computation.1 | async-start | bytes 10485760 | tf_op jit(solution)/shard_map/all_to_all | solution.py:60
  284.4 10.7 %copy-start.4 = (f32[2,16,40,768]{3,2,1,0:T(8,128)S(1)}, f32[2,16,40,768]{3,2,1,0:T(8,128)}, u32[]{:S(2)}) copy-start(f32[2,16,40,768]{3,2,1,0:T(8,128)} %copy-done.3) | copy-start | bytes 11796484
  399.3 119.8 %all-to-all-start.3 = ((bf16[16,2,40,2048]{3,2,1,0:T(8,128)(2,1)}), bf16[16,2,40,2048]{3,2,1,0:T(8,128)(2,1)}, u32[]{:S(2)}, u32[]{:S(2)}) async-start(bf16[16,2,40,2048]{3,2,1,0:T(8,128)(2,1)} %copy.43), calls=%async_computation.3 | async-start | bytes 10485760 | tf_op jit(solution)/shard_map/all_to_all | solution.py:63
  519.2 17.9 %copy-start.1 = (bf16[128,2048]{1,0:T(8,128)(2,1)S(1)}, bf16[128,2048]{1,0:T(8,128)(2,1)}, u32[]{:S(2)}) copy-start(bf16[128,2048]{1,0:T(8,128)(2,1)} %param.7) | copy-start | bytes 1572868
where the time goes:
time: 538 us; the launch traced here: 537 us
  waiting for transfers between devices  254 us (47%)
  blocking collectives  121 us (22%)
  matrix products  63.4 us (12%)
  local copies, waits for them, and re-layouts  54.3 us (10%)
  other arithmetic  27.6 us (5%)
  starting transfers between devices  15.2 us (3%)
    all_to_all x1, blocking collectives, shards(): lax.all_to_all(send_x, 'expert', split_axis=0, concat_axis=0, tiled=True)  121 us
    all_to_all x1, waiting for transfers between devices, shards(): lax.all_to_all(row_grad, 'expert', split_axis=0, concat_axis=0, tiled=True)  96.4 us
    all_to_all x1, waiting for transfers between devices, shards(): lax.all_to_all(send_grad, 'expert', split_axis=0, concat_axis=0, tiled=True)  85.3 us
    all_to_all x1, waiting for transfers between devices, shards(): lax.all_to_all(expert_out, 'expert', split_axis=0, concat_axis=0, tiled=T...  72.8 us
    gather x1, local copies, waits for them, and re-layouts, shards(): send_grad = jnp.where(filled[:, None], grad_rows[owner_row], 0)  13.6 us
    dot_general x1, matrix products, backward_part(): jnp.einsum('necf,edf->necd', gate_grad, w_gate, preferred_element_type=jn...  13.4 us
    dot_general x1, matrix products, backward_part(): jnp.einsum('necf,edf->necd', up_grad, w_up, preferred_element_type=jnp.fl...  12.3 us
    gather x1, local copies, waits for them, and re-layouts, shards(): grad_back = back_grad.reshape(-1, model_width)[slot_of].astype(jnp.float32)  12 us
  transfers between devices with their start and end apart: 3, of which 3 were waited for; matrix products, arithmetic and copies ran while one was open for 17% of the time, Pallas kernels for 0%

commit v1 on v0

v1 whole, which is shorter than its diff:
```python
import jax
import jax.numpy as jnp
from jax import lax
from jax.sharding import PartitionSpec as P

F32 = jnp.float32
BF16 = jnp.bfloat16


def shards(tokens, grad_out, routes, combine_weights, w_gate, w_up, w_down):
    nodes = lax.axis_size("expert")
    per_node = w_gate.shape[0]
    tok_rows, top_count = routes.shape
    width = tokens.shape[1]
    experts = per_node * nodes
    cap = 5 * tok_rows * top_count // (4 * experts)
    all_x = lax.all_gather(tokens, "expert")
    matches = routes[:, :, None] == jnp.arange(experts, dtype=jnp.int32)[None, None, :]
    dense = jnp.sum(jnp.where(matches, combine_weights[:, :, None], 0.0), axis=1)
    dense = dense.T.reshape(nodes, per_node, tok_rows)
    here = lax.all_to_all(dense, "expert", split_axis=0, concat_axis=0, tiled=True)
    all_g = lax.all_gather(grad_out, "expert")
    named = here > 0.0
    place = jnp.cumsum(named.astype(jnp.int32), axis=2) - 1
    pick = named[:, :, None, :] & (
        place[:, :, None, :] == jnp.arange(cap, dtype=jnp.int32)[None, None, :, None]
    )
    scale = jnp.sum(jnp.where(pick, here[:, :, None, :], 0.0), axis=3)
    scale = scale.transpose(1, 0, 2).reshape(per_node, nodes * cap, 1)
    hot = pick.astype(BF16).reshape(nodes, per_node * cap, tok_rows)

    def compact(rows):
        got = jnp.einsum("nct,ntd->ncd", hot, rows, preferred_element_type=F32).astype(BF16)
        got = got.reshape(nodes, per_node, cap, width).transpose(1, 0, 2, 3)
        return got.reshape(per_node, nodes * cap, width)

    def spread(rows):
        rows = rows.reshape(per_node, nodes, cap, width).transpose(1, 0, 2, 3)
        rows = rows.reshape(nodes, per_node * cap, width)
        got = jnp.einsum("nct,ncd->ntd", hot, rows, preferred_element_type=F32).astype(BF16)
        return lax.psum_scatter(got, "expert", scatter_dimension=0, tiled=False)

    x = compact(all_x)
    gate = jnp.einsum("erd,edf->erf", x, w_gate, preferred_element_type=F32)
    up = jnp.einsum("erd,edf->erf", x, w_up, preferred_element_type=F32)
    squash = jax.nn.sigmoid(gate)
    act = gate * squash
    hidden = act * up
    out = jnp.einsum(
        "erf,efd->erd", (hidden * scale).astype(BF16), w_down, preferred_element_type=F32
    ).astype(BF16)
    combined = spread(out)
    g = compact(all_g)
    pull = jnp.einsum("erd,efd->erf", g, w_down, preferred_element_type=F32)
    dots = jnp.sum(pull * hidden, axis=2).reshape(per_node, nodes, cap).transpose(1, 0, 2)
    dots = jnp.sum(jnp.where(pick, dots[:, :, :, None], 0.0), axis=2)
    back = lax.all_to_all(dots, "expert", split_axis=0, concat_axis=0, tiled=True)
    back = back.reshape(experts, tok_rows).T
    grad_weights = jnp.sum(jnp.where(matches, back[:, None, :], 0.0), axis=2)
    pull = pull * scale
    gate_grad = (pull * up * squash * (1.0 + gate * (1.0 - squash))).astype(BF16)
    up_grad = (pull * act).astype(BF16)
    row_grad = jnp.einsum("erf,edf->erd", gate_grad, w_gate, preferred_element_type=F32)
    row_grad = row_grad + jnp.einsum("erf,edf->erd", up_grad, w_up, preferred_element_type=F32)
    grad_tokens = spread(row_grad.astype(BF16))
    return (combined, grad_tokens, grad_weights)


def solution(mesh):
    rows = P(("groups", "expert"), None)
    held = P("expert", None, None)
    return jax.shard_map(
        shards,
        mesh=mesh,
        in_specs=(rows, rows, rows, rows, held, held, held),
        out_specs=(rows, rows, rows),
        check_vma=False,
    )
```

time: 538 us -> 434 us (0.81)
  the two profiles are of different devices: /device:TPU:13 before, /device:TPU:0 now
where the time goes in v1:
time: 434 us
  waiting for transfers between devices  302 us (70%)
  matrix products  86.6 us (20%)
  between operations  13.9 us (3%)
  local copies, waits for them, and re-layouts  10.9 us (3%)
  blocking collectives  10.2 us (2%)
  starting transfers between devices  7.54 us (2%)
    reduce_scatter x2, waiting for transfers between devices, spread(): return lax.psum_scatter(got, 'expert', scatter_dimension=0, tiled=False)  163 us
    all_gather x1, waiting for transfers between devices, shards(): all_x = lax.all_gather(tokens, 'expert')  68.1 us
    all_gather x1, waiting for transfers between devices, shards(): all_g = lax.all_gather(grad_out, 'expert')  63.1 us
    dot_general x1, matrix products, shards(): jnp.einsum('erf,edf->erd', gate_grad, w_gate, preferred_element_type=F32)  16.9 us
    dot_general x1, matrix products, shards(): jnp.einsum('erf,edf->erd', up_grad, w_up, preferred_element_type=F32)  13 us
    dot_general x2, matrix products, compact(): jnp.einsum('nct,ntd->ncd', hot, rows, preferred_element_type=F32)  12.1 us
    dot_general x2, matrix products, spread(): jnp.einsum('nct,ncd->ntd', hot, rows, preferred_element_type=F32)  11.5 us
    dot_general x1, matrix products, shards(): pull = jnp.einsum('erd,efd->erf', g, w_down, preferred_element_type=F32)  10.4 us
  transfers between devices with their start and end apart: 5, of which 5 were waited for; matrix products, arithmetic and copies ran while one was open for 11% of the time, Pallas kernels for 0%

profile of v1, /device:TPU:0, one launch (start us, length us, event | category | flops | bytes accessed | tf_op | source)
XLA Modules:
  0.0 434.0 jit_solution(4407872243625463056)
XLA Ops:
  7.2 0.0 all-gather.7.cloned.1.call-start
  7.2 0.7 all-gather.7.cloned.1.call-update
  7.9 0.0 all-gather.5.cloned.1.call-start
  7.9 0.7 all-gather.5.cloned.1.call-update
  8.6 1.3 select_reduce_fusion.3
  10.0 7.4 %all-to-all-start = ((f32[16,2,128]{2,1,0:T(2,128)}), f32[16,2,128]{2,1,0:T(2,128)S(1)}, u32[]{:S(2)}, u32[]{:S(2)}) async-start(f32[16,2,128]{2,1,0:T(2,128)} %bitcast.1), calls=%async_computation | async-start | bytes 32768 | tf_op jit(solution)/shard_map/all_to_all | solution.py:21
  17.4 0.0 reduce-scatter.3.cloned.1.call-start
  17.4 0.1 eq.43
  17.5 6.4 %all-to-all-done = f32[16,2,128]{2,1,0:T(2,128)S(1)} async-done(((f32[16,2,128]{2,1,0:T(2,128)}), f32[16,2,128]{2,1,0:T(2,128)S(1)}, u32[]{:S(2)}, u32[]{:S(2)}) %all-to-all-start) | async-done | bytes 16416 | tf_op jit(solution)/shard_map/all_to_all | solution.py:21
  23.9 0.6 reduce_window_sum.11
  24.5 0.2 fusion.8
  24.7 63.1 %all-gather.7.cloned.1.call-done = bf16[2048,2048]{1,0:T(8,128)(2,1)} async-done(((bf16[128,2048]{1,0:T(8,128)(2,1)}), bf16[2048,2048]{1,0:T(8,128)(2,1)}) %all-gather.7.cloned.1.call-update) | async-done | bytes 8388624 | tf_op jit(solution)/shard_map/all_gather | solution.py:22
  87.8 7.2 %convolution_convert_fusion.2 = bf16[16,80,2048]{2,1,0:T(8,128)(2,1)} fusion(pred[16,80,128]{2,1,0:T(8,128)(4,1)S(1)} %fusion.8, bf16[16,128,2048]{2,1,0:T(8,128)(2,1)} %bitcast.53), kind=kOutput, calls=%fused_computation.3 | convolution fusion | flops 673710080 | bytes 13795328 | tf_op jit(solution)/shard_map/nct,ntd->ncd/dot_general | solution.py:33
  95.0 68.1 %all-gather.5.cloned.1.call-done = bf16[2048,2048]{1,0:T(8,128)(2,1)} async-done(((bf16[128,2048]{1,0:T(8,128)(2,1)}), bf16[2048,2048]{1,0:T(8,128)(2,1)}) %all-gather.5.cloned.1.call-update) | async-done | bytes 8388624 | tf_op jit(solution)/shard_map/all_gather | solution.py:17
  163.1 4.9 %convolution_convert_fusion.4 = bf16[16,80,2048]{2,1,0:T(8,128)(2,1)S(1)} fusion(pred[16,80,128]{2,1,0:T(8,128)(4,1)S(1)} %fusion.8, bf16[16,128,2048]{2,1,0:T(8,128)(2,1)} %bitcast.54), kind=kOutput, calls=%fused_computation.5 | convolution fusion | flops 673710080 | bytes 13795328 | tf_op jit(solution)/shard_map/nct,ntd->ncd/dot_general | solution.py:33
  168.0 0.0 copy-start
  168.0 3.1 copy.71
  171.1 1.3 copy-done
  172.4 0.0 copy-start.1
  172.4 0.0 slice-start
  172.4 0.4 copy.74
  172.9 2.0 copy-done.1
  174.9 0.0 slice-start.1
  174.9 6.6 %fusion.13 = f32[2,640,768]{2,1,0:T(8,128)S(1)} fusion(bf16[2,640,2048]{2,1,0:T(8,128)(2,1)S(1)} %bitcast.58, bf16[2,2048,768]{2,1,0:T(8,128)(2,1)} %param.11), kind=kOutput, calls=%fused_computation.31 | convolution fusion | flops 4026531840 | bytes 15466496 | tf_op jit(solution)/shard_map/erd,edf->erf/dot_general | solution.py:44
  181.5 0.0 slice-done
  181.6 0.0 slice-done.1
  181.6 0.0 copy-start.3
  181.6 6.2 %fusion.14 = f32[2,640,768]{2,1,0:T(8,128)} fusion(bf16[2,640,2048]{2,1,0:T(8,128)(2,1)S(1)} %bitcast.59, bf16[2,2048,768]{2,1,0:T(8,128)(2,1)S(1)} %bitcast.66), kind=kOutput, calls=%fused_computation.32 | convolution fusion | flops 4026531840 | bytes 15466496 | tf_op jit(solution)/shard_map/erd,edf->erf/dot_general | solution.py:45
  187.7 0.0 copy-done.3
  187.7 10.4 %multiply_reduce_fusion = (f32[2,640]{1,0:T(2,128)S(1)}, f32[2,640,768]{2,1,0:T(8,128)}) fusion(f32[2,640,768]{2,1,0:T(8,128)} %fusion.14, f32[2,640,768]{2,1,0:T(8,128)S(1)} %fusion.13, bf16[2,640,2048]{2,1,0:T(8,128)(2,1)S(1)} %bitcast.57, bf16[2,768,2048]{2,1,0:T(8,128)(2,1)} %param.13), kind=kOutput, calls=%fused_computation.6 | convolution fusion | flops 4033411840 | bytes 23335936 | tf_op jit(solution)/shard_map/erd,efd->erf/dot_general | solution.py:54
  198.1 0.1 reshape.67
  198.3 0.6 select_reduce_fusion
  198.8 0.1 mul.42
  198.9 9.9 %convolution_convert_fusion.3 = bf16[2,640,2048]{2,1,0:T(8,128)(2,1)S(1)} fusion(bf16[2,768,2048]{2,1,0:T(8,128)(2,1)} %param.13, f32[2,640]{1,0:T(2,128)S(1)} %mul.42, f32[2,640,768]{2,1,0:T(8,128)} %fusion.14, f32[2,640,768]{2,1,0:T(8,128)} %copy-done.3), kind=kOutput, calls=%fused_computation.4 | convolution fusion | flops 4036034560 | bytes 19403776 | tf_op jit(solution)/shard_map/erf,efd->erd/dot_general | solution.py:49
  208.9 0.4 copy.73
  209.3 6.0 %convolution_convert_fusion.1 = bf16[16,128,2048]{2,1,0:T(8,128)(2,1)} fusion(pred[16,80,128]{2,1,0:T(8,128)(4,1)S(1)} %fusion.8, bf16[16,80,2048]{2,1,0:T(8,128)(2,1)S(1)} %bitcast.56), kind=kOutput, calls=%fused_computation.2 | convolution fusion | flops 675282944 | bytes 13795328 | tf_op jit(solution)/shard_map/nct,ncd->ntd/dot_general | solution.py:40
  215.3 0.0 reduce-scatter.3.cloned.1.call-update
  215.3 0.0 reduce-scatter.5.cloned.1.call-start
  215.3 16.9 %fusion.1 = f32[2,640,2048]{2,1,0:T(8,128)} fusion(bf16[2,2048,768]{2,1,0:T(8,128)(2,1)} %param.11, f32[2,640,768]{2,1,0:T(8,128)} %copy-done.3, f32[2,640,768]{2,1,0:T(8,128)} %fusion.14, f32[2,640,768]{2,1,0:T(8,128)} %get-tuple-element.8, f32[2,640]{1,0:T(2,128)S(1)} %mul.42), kind=kOutput, calls=%fused_computation.12 | convolution fusion | flops 4037345280 | bytes 28578816 | tf_op jit(solution)/shard_map/erf,edf->erd/dot_general | solution.py:63
  232.2 13.0 %add_convert_fusion = bf16[2,640,2048]{2,1,0:T(8,128)(2,1)} fusion(f32[2,640,2048]{2,1,0:T(8,128)} %fusion.1, bf16[2,2048,768]{2,1,0:T(8,128)(2,1)} %param.12, f32[2,640,768]{2,1,0:T(8,128)} %get-tuple-element.8, f32[2,640]{1,0:T(2,128)S(1)} %mul.42, f32[2,640,768]{2,1,0:T(8,128)} %copy-done.3), kind=kOutput, calls=%fused_computation | convolution fusion | flops 4038656000 | bytes 29889536 | tf_op jit(solution)/shard_map/erf,edf->erd/dot_general | solution.py:64
  245.2 3.3 copy.75
  248.5 5.6 %convolution_convert_fusion = bf16[16,128,2048]{2,1,0:T(8,128)(2,1)} fusion(pred[16,80,128]{2,1,0:T(8,128)(4,1)S(1)} %fusion.8, bf16[16,80,2048]{2,1,0:T(8,128)(2,1)S(1)} %bitcast.55), kind=kOutput, calls=%fused_computation.1 | convolution fusion | flops 675282944 | bytes 13795328 | tf_op jit(solution)/shard_map/nct,ncd->ntd/dot_general | solution.py:40
  254.1 0.0 copy-start.2
  254.1 0.0 reduce-scatter.5.cloned.1.call-update
  254.1 10.2 %all_to_all.10 = f32[16,2,128]{2,1,0:T(2,128)S(1)} all-to-all(f32[16,2,128]{2,1,0:T(2,128)S(1)} %get-tuple-element.3), channel_id=1, replica_groups=mesh['groups'=2,'expert'=16] {'expert'}, dimensions={0} | all-to-all | bytes 32768 | tf_op jit(solution)/shard_map/all_to_all | solution.py:57
  264.2 0.0 copy-done.2
  264.2 0.6 select_reduce_fusion.2
  264.9 53.8 %reduce-scatter.3.cloned.1.call-done = bf16[1,128,2048]{2,1,0:T(8,128)(2,1)} async-done(((bf16[16,128,2048]{2,1,0:T(8,128)(2,1)}), bf16[1,128,2048]{2,1,0:T(8,128)(2,1)}) %reduce-scatter.3.cloned.1.call-update) | async-done | bytes 524304 | tf_op jit(solution)/shard_map/reduce_scatter | solution.py:41
  318.6 108.9 %reduce-scatter.5.cloned.1.call-done = bf16[1,128,2048]{2,1,0:T(8,128)(2,1)} async-done(((bf16[16,128,2048]{2,1,0:T(8,128)(2,1)}), bf16[1,128,2048]{2,1,0:T(8,128)(2,1)}) %reduce-scatter.5.cloned.1.call-update) | async-done | bytes 524304 | tf_op jit(solution)/shard_map/reduce_scatter | solution.py:41
  (8 shorter events, 0.1 us)
Async XLA Ops:
  7.2 80.6 %all-gather.7.cloned.1.call-start = ((), (), s32[]{:S(2)}) async-start(), calls=%async_computation.7 | async-start | bytes 8912896 | tf_op jit(solution)/shard_map/all_gather | solution.py:22
  7.9 155.2 %all-gather.5.cloned.1.call-start = ((), (), s32[]{:S(2)}) async-start(), calls=%async_computation.6 | async-start | bytes 8912896 | tf_op jit(solution)/shard_map/all_gather | solution.py:17
  10.0 13.9 %all-to-all-start = ((f32[16,2,128]{2,1,0:T(2,128)}), f32[16,2,128]{2,1,0:T(2,128)S(1)}, u32[]{:S(2)}, u32[]{:S(2)}) async-start(f32[16,2,128]{2,1,0:T(2,128)} %bitcast.1), calls=%async_computation | async-start | bytes 32768 | tf_op jit(solution)/shard_map/all_to_all | solution.py:21
  17.4 301.3 %reduce-scatter.3.cloned.1.call-start = ((), (), s32[]{:S(2)}) async-start(), calls=%async_computation.4 | async-start | bytes 8912896 | tf_op jit(solution)/shard_map/reduce_scatter | solution.py:41
  168.0 4.4 %copy-start = (bf16[16,80,2048]{2,1,0:T(8,128)(2,1)S(1)}, bf16[16,80,2048]{2,1,0:T(8,128)(2,1)}, u32[]{:S(2)}) copy-start(bf16[16,80,2048]{2,1,0:T(8,128)(2,1)} %convolution_convert_fusion.2) | copy-start | bytes 15728644
  172.4 2.5 copy-start.1
  172.4 9.1 %slice-start = ((s8[6291456]{0:T(1024)(128)(4,1)}), s8[2097152]{0:T(1024)(128)(4,1)S(1)}, s32[]{:S(2)}) async-start(s8[6291456]{0:T(1024)(128)(4,1)} %bitcast.65), calls=%async_computation.8 | async-start | bytes 4194304
  174.9 6.7 %slice-start.1 = ((s8[6291456]{0:T(1024)(128)(4,1)}), s8[4194304]{0:T(1024)(128)(4,1)S(1)}, s32[]{:S(2)}) async-start(s8[6291456]{0:T(1024)(128)(4,1)} %bitcast.65), calls=%async_computation.9 | async-start | bytes 8388608
  181.6 6.2 %copy-start.3 = (f32[2,640,768]{2,1,0:T(8,128)}, f32[2,640,768]{2,1,0:T(8,128)S(1)}, u32[]{:S(2)}) copy-start(f32[2,640,768]{2,1,0:T(8,128)S(1)} %fusion.13) | copy-start | bytes 11796484
  215.3 212.2 %reduce-scatter.5.cloned.1.call-start = ((), (), s32[]{:S(2)}) async-start(), calls=%async_computation.5 | async-start | bytes 8912896 | tf_op jit(solution)/shard_map/reduce_scatter | solution.py:41
  254.1 10.2 %copy-start.2 = (s32[128,8]{0,1:T(8,128)S(1)}, s32[128,8]{0,1:T(8,128)}, u32[]{:S(2)}) copy-start(s32[128,8]{0,1:T(8,128)} %param.9) | copy-start | bytes 12292
Sparse Core Ops, SparseCore 0:
  10.2 77.5 all-gather.6
  89.9 73.1 all-gather.4
  215.4 103.1 reduce-scatter.2
  323.1 104.3 reduce-scatter.4

commit v2 on v1

--- a/solution.py
+++ b/solution.py
@@ -1,10 +1,41 @@
 import jax
 import jax.numpy as jnp
+import numpy as np
 from jax import lax
 from jax.sharding import PartitionSpec as P
 
 F32 = jnp.float32
 BF16 = jnp.bfloat16
+
+
+def ring_order(chips):
+    if chips == 8:
+        return [0, 2, 4, 6, 7, 5, 3, 1]
+    return list(range(chips))
+
+
+def plan(nodes):
+    chips = nodes // 2
+    order = ring_order(chips)
+    at = {chip: i for i, chip in enumerate(order)}
+
+    def moves(step):
+        return [
+            (order[i] * 2 + c, order[(i + step) % chips] * 2 + c)
+            for i in range(chips)
+            for c in range(2)
+        ]
+
+    swap = [(i, i ^ 1) for i in range(nodes)]
+    half = chips // 2
+    groups = [[0]] + [[d, chips - d] for d in range(1, half)] + [[half]]
+    slots = [(d, k) for group in groups for d in group for k in range(2)]
+    table = np.zeros((nodes, nodes), np.int32)
+    for me in range(nodes):
+        for j, (d, k) in enumerate(slots):
+            table[me, j] = order[(at[me // 2] - d) % chips] * 2 + ((me % 2) ^ k)
+    inverse = np.argsort(table, axis=1).astype(np.int32)
+    return half, groups, moves(1), moves(-1), swap, table, inverse
 
 
 def shards(tokens, grad_out, routes, combine_weights, w_gate, w_up, w_down):
@@ -14,12 +45,34 @@
     width = tokens.shape[1]
     experts = per_node * nodes
     cap = 5 * tok_rows * top_count // (4 * experts)
-    all_x = lax.all_gather(tokens, "expert")
+    mid = tok_rows // 2
+    half, groups, right, left, swap, table, inverse = plan(nodes)
+    me = lax.axis_index("expert")
+
+    def go_right(rows):
+        return lax.ppermute(rows, "expert", right)
+
+    def go_left(rows):
+        return lax.ppermute(rows, "expert", left)
+
+    def across(rows):
+        return lax.ppermute(rows, "expert", swap)
+
+    def gather_ring(own, after=None):
+        rings, last = [[own]], None
+        from_left, from_right = own, own
+        for _ in range(1, half):
+            from_left, from_right = go_right(from_left), go_left(from_right)
+            rings.append([from_left, from_right])
+        last = jnp.concatenate([go_right(from_left[:mid]), go_left(from_right[mid:])], axis=0)
+        rings.append([last])
+        return rings, (from_left, from_right)
+
     matches = routes[:, :, None] == jnp.arange(experts, dtype=jnp.int32)[None, None, :]
     dense = jnp.sum(jnp.where(matches, combine_weights[:, :, None], 0.0), axis=1)
     dense = dense.T.reshape(nodes, per_node, tok_rows)
     here = lax.all_to_all(dense, "expert", split_axis=0, concat_axis=0, tiled=True)
-    all_g = lax.all_gather(grad_out, "expert")
+    here = here[jnp.asarray(table)[me]]
     named = here > 0.0
     place = jnp.cumsum(named.astype(jnp.int32), axis=2) - 1
     pick = named[:, :, None, :] & (
@@ -29,18 +82,46 @@
     scale = scale.transpose(1, 0, 2).reshape(per_node, nodes * cap, 1)
     hot = pick.astype(BF16).reshape(nodes, per_node * cap, tok_rows)
 
-    def compact(rows):
-        got = jnp.einsum("nct,ntd->ncd", hot, rows, preferred_element_type=F32).astype(BF16)
-        got = got.reshape(nodes, per_node, cap, width).transpose(1, 0, 2, 3)
-        return got.reshape(per_node, nodes * cap, width)
+    starts = np.cumsum([0] + [2 * len(group) for group in groups])
+
+    def compact(rings):
+        parts = []
+        for number, ring in enumerate(rings):
+            rows = jnp.stack([r for own in ring for r in (own, across(own))])
+            span = slice(int(starts[number]), int(starts[number + 1]))
+            got = jnp.einsum("nct,ntd->ncd", hot[span], rows, preferred_element_type=F32)
+            got = got.astype(BF16).reshape(-1, per_node, cap, width)
+            parts.append(got.transpose(1, 0, 2, 3).reshape(per_node, -1, width))
+        return jnp.concatenate(parts, axis=1)
 
     def spread(rows):
-        rows = rows.reshape(per_node, nodes, cap, width).transpose(1, 0, 2, 3)
-        rows = rows.reshape(nodes, per_node * cap, width)
-        got = jnp.einsum("nct,ncd->ntd", hot, rows, preferred_element_type=F32).astype(BF16)
-        return lax.psum_scatter(got, "expert", scatter_dimension=0, tiled=False)
+        rows = rows.reshape(per_node, nodes, cap, width)
 
-    x = compact(all_x)
+        def partials(number):
+            span = slice(int(starts[number]), int(starts[number + 1]))
+            part = rows[:, span].transpose(1, 0, 2, 3).reshape(-1, per_node * cap, width)
+            got = jnp.einsum("nct,ncd->ntd", hot[span], part, preferred_element_type=F32)
+            return [
+                got[2 * i] + across(got[2 * i + 1].astype(BF16)).astype(F32)
+                for i in range(len(groups[number]))
+            ]
+
+        far = partials(half)[0].astype(BF16)
+        to_left, to_right = go_left(far[:mid]), go_right(far[mid:])
+        blank = jnp.zeros((tok_rows - mid, width), BF16)
+        to_left = jnp.concatenate([to_left, blank], axis=0)
+        to_right = jnp.concatenate([blank, to_right], axis=0)
+        for number in range(half - 1, 0, -1):
+            near, other = partials(number)
+            to_left = go_left((near + to_left.astype(F32)).astype(BF16))
+            to_right = go_right((other + to_right.astype(F32)).astype(BF16))
+        total = partials(0)[0] + to_left.astype(F32) + to_right.astype(F32)
+        return total.astype(BF16)
+
+    rings, ends = gather_ring(tokens)
+    x = compact(rings)
+    grad_out, _ = lax.optimization_barrier((grad_out, ends))
+    rings, _ = gather_ring(grad_out)
     gate = jnp.einsum("erd,edf->erf", x, w_gate, preferred_element_type=F32)
     up = jnp.einsum("erd,edf->erf", x, w_up, preferred_element_type=F32)
     squash = jax.nn.sigmoid(gate)
@@ -50,10 +131,11 @@
         "erf,efd->erd", (hidden * scale).astype(BF16), w_down, preferred_element_type=F32
     ).astype(BF16)
     combined = spread(out)
-    g = compact(all_g)
+    g = compact(rings)
     pull = jnp.einsum("erd,efd->erf", g, w_down, preferred_element_type=F32)
     dots = jnp.sum(pull * hidden, axis=2).reshape(per_node, nodes, cap).transpose(1, 0, 2)
     dots = jnp.sum(jnp.where(pick, dots[:, :, :, None], 0.0), axis=2)
+    dots = dots[jnp.asarray(inverse)[me]]
     back = lax.all_to_all(dots, "expert", split_axis=0, concat_axis=0, tiled=True)
     back = back.reshape(experts, tok_rows).T
     grad_weights = jnp.sum(jnp.where(matches, back[:, None, :], 0.0), axis=2)

time: 434 us -> 310 us (0.71); the launches traced: 434 us -> 305 us
  waiting for transfers between devices: 302 us -> 134 us
  starting transfers between devices: 7.54 us -> 51.4 us
  between operations: 13.9 us -> 1.84 us
  local copies, waits for them, and re-layouts: 10.9 us -> 22.9 us
  blocking collectives: 10.2 us -> 0 us
  other arithmetic: 3.27 us -> 12.9 us
    reduce_scatter x2 -> x0, waiting for transfers between devices: 163 us -> none  [spread(): return lax.psum_scatter(got, 'expert', scatter_dimension=0, tiled=False)]
    all_gather x2 -> x0, waiting for transfers between devices: 131 us -> none  [the longest x1 68.1 us: shards(): all_x = lax.all_gather(tokens, 'expert')]
    ppermute x0 -> x64, waiting for transfers between devices: none -> 121 us  [the longest x16 76.7 us: go_left(): return lax.ppermute(rows, 'expert', left)]
    ppermute x0 -> x64, starting transfers between devices: none -> 41.5 us  [the longest x16 20.2 us: go_left(): return lax.ppermute(rows, 'expert', left)]
    convert_element_type x0 -> x10, local copies, waits for them, and re-layouts: none -> 10.2 us  [partials(): got[2 * i + 1].astype(BF16)]
    all_to_all x1 -> x0, blocking collectives: 10.2 us -> none  [shards(): lax.all_to_all(dots, 'expert', split_axis=0, concat_axis=0, tiled=True)]
    convert_element_type x0 -> x10, other arithmetic: none -> 8.87 us  [the longest x6 4.02 us: spread(): to_left = go_left((near + to_left.astype(F32)).astype(BF16))]
    dot_general x4 -> x20, matrix products: 23.6 us -> 25.4 us  [the longest x10 19.9 us: partials(): jnp.einsum('nct,ncd->ntd', hot[span], part, preferred_element_type=F32)]
  transfers between devices with their start and end apart: 5 -> 66, of which waited for: 5 -> 24; matrix products, arithmetic and copies ran while one was open for 11% -> 20% of each run, Pallas kernels for 0% -> 0%
where the time goes in v2:
time: 310 us; the launch traced here: 305 us
  waiting for transfers between devices  134 us (43%)
  matrix products  82.4 us (27%)
  starting transfers between devices  51.4 us (17%)
  local copies, waits for them, and re-layouts  22.9 us (7%)
  other arithmetic  12.9 us (4%)
    ppermute x16, waiting for transfers between devices, go_left(): return lax.ppermute(rows, 'expert', left)  76.7 us
    ppermute x16, waiting for transfers between devices, go_right(): return lax.ppermute(rows, 'expert', right)  42.6 us
    ppermute x16, starting transfers between devices, go_left(): return lax.ppermute(rows, 'expert', left)  20.2 us
    dot_general x10, matrix products, partials(): jnp.einsum('nct,ncd->ntd', hot[span], part, preferred_element_type=F32)  19.9 us
    dot_general x1, matrix products, shards(): jnp.einsum('erf,edf->erd', gate_grad, w_gate, preferred_element_type=F32)  15.5 us
    ppermute x16, starting transfers between devices, go_right(): return lax.ppermute(rows, 'expert', right)  15.2 us
    dot_general x1, matrix products, shards(): jnp.einsum('erf,edf->erd', up_grad, w_up, preferred_element_type=F32)  11 us
    dot_general x1, matrix products, shards(): pull = jnp.einsum('erd,efd->erf', g, w_down, preferred_element_type=F32)  10.3 us
  transfers between devices with their start and end apart: 66, of which 24 were waited for; matrix products, arithmetic and copies ran while one was open for 20% of the time, Pallas kernels for 0%

profile of v2, /device:TPU:0, one launch (start us, length us, event | category | flops | bytes accessed | tf_op | source)
XLA Modules:
  0.0 305.2 jit_solution(8470306555759120178)
XLA Ops:
  0.6 3.0 collective-permute-start.3
  3.8 1.3 select_reduce_fusion.3
  5.1 6.4 %all-to-all-start = ((f32[16,2,128]{2,1,0:T(2,128)}), f32[16,2,128]{2,1,0:T(2,128)S(1)}, u32[]{:S(2)}, u32[]{:S(2)}) async-start(f32[16,2,128]{2,1,0:T(2,128)} %bitcast.1), calls=%async_computation | async-start | bytes 32768 | tf_op jit(solution)/shard_map/all_to_all | solution.py:74
  12.3 8.3 %all-to-all-done = f32[16,2,128]{2,1,0:T(2,128)S(1)} async-done(((f32[16,2,128]{2,1,0:T(2,128)}), f32[16,2,128]{2,1,0:T(2,128)S(1)}, u32[]{:S(2)}, u32[]{:S(2)}) %all-to-all-start) | async-done | bytes 16416 | tf_op jit(solution)/shard_map/all_to_all | solution.py:74
  22.5 1.6 collective-permute-start.7
  24.3 1.4 convolution_convert_fusion.10
  25.8 9.8 %collective-permute-done.5 = bf16[128,2048]{1,0:T(8,128)(2,1)S(1)} collective-permute-done((bf16[128,2048]{1,0:T(8,128)(2,1)S(1)}, bf16[128,2048]{1,0:T(8,128)(2,1)S(1)}, u32[]{:S(2)}, u32[]{:S(2)}) %collective-permute-start.5) | collective-permute-done | bytes 524320 | tf_op jit(solution)/shard_map/ppermute | solution.py:53
  36.8 1.6 collective-permute-start.11
  39.1 11.6 %collective-permute-done.11 = bf16[128,2048]{1,0:T(8,128)(2,1)S(1)} collective-permute-done((bf16[128,2048]{1,0:T(8,128)(2,1)S(1)}, bf16[128,2048]{1,0:T(8,128)(2,1)S(1)}, u32[]{:S(2)}, u32[]{:S(2)}) %collective-permute-start.11) | collective-permute-done | bytes 524320 | tf_op jit(solution)/shard_map/ppermute | solution.py:56
  52.3 1.8 collective-permute-start.14
  54.7 14.7 %collective-permute-done.13 = bf16[64,2048]{1,0:T(8,128)(2,1)S(1)} collective-permute-done((bf16[64,2048]{1,0:T(8,128)(2,1)S(1)}, bf16[64,2048]{1,0:T(8,128)(2,1)S(1)}, u32[]{:S(2)}, u32[]{:S(2)}) %collective-permute-start.13) | collective-permute-done | bytes 262176 | tf_op jit(solution)/shard_map/ppermute | solution.py:53
  73.0 1.2 collective-permute-start.37
  74.2 7.4 %collective-permute-done.35 = bf16[128,2048]{1,0:T(8,128)(2,1)S(1)} collective-permute-done((bf16[128,2048]{1,0:T(8,128)(2,1)S(1)}, bf16[128,2048]{1,0:T(8,128)(2,1)S(1)}, u32[]{:S(2)}, u32[]{:S(2)}) %collective-permute-start.35) | collective-permute-done | bytes 524320 | tf_op jit(solution)/shard_map/ppermute | solution.py:56
  82.9 4.3 %fusion.140 = f32[2,640,768]{2,1,0:T(8,128)S(1)} fusion(bf16[2,640,2048]{2,1,0:T(8,128)(2,1)S(1)} %constant_dynamic-update-slice_fusion.2, bf16[2,2048,768]{2,1,0:T(8,128)(2,1)S(1)} %bitcast.394), kind=kOutput, calls=%fused_computation.225 | convolution fusion | flops 4026531840 | bytes 15466496 | tf_op jit(solution)/shard_map/erd,edf->erf/dot_general | solution.py:125
  87.2 6.2 %fusion.141 = f32[2,640,768]{2,1,0:T(8,128)} fusion(bf16[2,640,2048]{2,1,0:T(8,128)(2,1)S(1)} %constant_dynamic-update-slice_fusion.2, bf16[2,2048,768]{2,1,0:T(8,128)(2,1)S(1)} %bitcast.396), kind=kOutput, calls=%fused_computation.226 | convolution fusion | flops 4026531840 | bytes 15466496 | tf_op jit(solution)/shard_map/erd,edf->erf/dot_general | solution.py:126
  93.6 1.6 collective-permute-start.41
  97.4 10.3 %collective-permute-done.41 = bf16[128,2048]{1,0:T(8,128)(2,1)S(1)} collective-permute-done((bf16[128,2048]{1,0:T(8,128)(2,1)S(1)}, bf16[128,2048]{1,0:T(8,128)(2,1)S(1)}, u32[]{:S(2)}, u32[]{:S(2)}) %collective-permute-start.41) | collective-permute-done | bytes 524320 | tf_op jit(solution)/shard_map/ppermute | solution.py:53
  107.7 1.7 collective-permute-start.45
  110.1 1.2 collective-permute-done.43
  112.7 2.7 collective-permute-done.45
  115.5 4.1 %collective-permute-done.46 = bf16[64,2048]{1,0:T(8,128)(2,1)S(1)} collective-permute-done((bf16[64,2048]{1,0:T(8,128)(2,1)S(1)}, bf16[64,2048]{1,0:T(8,128)(2,1)S(1)}, u32[]{:S(2)}, u32[]{:S(2)}) %collective-permute-start.46) | collective-permute-done | bytes 262176 | tf_op jit(solution)/shard_map/ppermute | solution.py:56
  120.5 1.1 collective-permute-done.47
  122.1 10.3 %multiply_reduce_fusion = (f32[2,640]{1,0:T(2,128)S(1)}, f32[2,640,768]{2,1,0:T(8,128)}) fusion(f32[2,640,768]{2,1,0:T(8,128)} %fusion.141, f32[2,640,768]{2,1,0:T(8,128)S(1)} %fusion.140, bf16[2,640,2048]{2,1,0:T(8,128)(2,1)S(1)} %constant_dynamic-update-slice_fusion.9, bf16[2,768,2048]{2,1,0:T(8,128)(2,1)} %param.15), kind=kOutput, calls=%fused_computation.4 | convolution fusion | flops 4033411840 | bytes 23335936 | tf_op jit(solution)/shard_map/erd,efd->erf/dot_general | solution.py:135
  133.2 15.5 %fusion.43 = f32[2,640,2048]{2,1,0:T(8,128)} fusion(bf16[2,2048,768]{2,1,0:T(8,128)(2,1)} %param.13, f32[2,640,768]{2,1,0:T(8,128)} %copy-done.21, f32[2,640,768]{2,1,0:T(8,128)} %fusion.141, f32[2,640,768]{2,1,0:T(8,128)} %get-tuple-element.53, f32[2,640]{1,0:T(2,128)S(1)} %mul.42), kind=kOutput, calls=%fused_computation.62 | convolution fusion | flops 4037345280 | bytes 28578816 | tf_op jit(solution)/shard_map/erf,edf->erd/dot_general | solution.py:145
  148.7 11.0 %add_convert_fusion = bf16[2,640,2048]{2,1,0:T(8,128)(2,1)S(1)} fusion(f32[2,640,2048]{2,1,0:T(8,128)} %fusion.43, bf16[2,2048,768]{2,1,0:T(8,128)(2,1)} %param.14, f32[2,640,768]{2,1,0:T(8,128)} %get-tuple-element.53, f32[2,640]{1,0:T(2,128)S(1)} %mul.42, f32[2,640,768]{2,1,0:T(8,128)} %copy-done.21), kind=kOutput, calls=%fused_computation.2 | convolution fusion | flops 4038656000 | bytes 29889536 | tf_op jit(solution)/shard_map/erf,edf->erd/dot_general | solution.py:146
  159.7 1.2 slice_bitcast_fusion.22
  160.8 1.3 slice_bitcast_fusion
  162.2 9.8 %convolution_convert_fusion = bf16[2,640,2048]{2,1,0:T(8,128)(2,1)S(1)} fusion(bf16[2,768,2048]{2,1,0:T(8,128)(2,1)} %param.15, f32[2,640]{1,0:T(2,128)S(1)} %mul.42, f32[2,640,768]{2,1,0:T(8,128)} %fusion.141, f32[2,640,768]{2,1,0:T(8,128)} %copy-done.21), kind=kOutput, calls=%fused_computation.3 | convolution fusion | flops 4036034560 | bytes 19403776 | tf_op jit(solution)/shard_map/erf,efd->erd/dot_general | solution.py:130
  173.7 1.3 copy-done.7
  176.1 2.8 fusion.137
  180.6 2.8 fusion.138
  185.0 2.8 fusion.139
  190.0 1.3 copy-done.8
  192.4 2.8 fusion.134
  196.3 2.8 fusion.135
  200.2 2.7 fusion.136
  204.1 1.8 fusion.142
  205.9 1.2 gather_fusion.1
  207.1 3.5 %all-to-all-start.1 = ((f32[16,2,128]{2,1,0:T(2,128)}), f32[16,2,128]{2,1,0:T(2,128)S(1)}, u32[]{:S(2)}, u32[]{:S(2)}) async-start(f32[16,2,128]{2,1,0:T(2,128)} %gather_fusion.1), calls=%async_computation.1 | async-start | bytes 32768 | tf_op jit(solution)/shard_map/all_to_all | solution.py:139
  210.6 2.1 fusion.110
  212.7 4.3 %all-to-all-done.1 = f32[16,2,128]{2,1,0:T(2,128)S(1)} async-done(((f32[16,2,128]{2,1,0:T(2,128)}), f32[16,2,128]{2,1,0:T(2,128)S(1)}, u32[]{:S(2)}, u32[]{:S(2)}) %all-to-all-start.1) | async-done | bytes 16416 | tf_op jit(solution)/shard_map/all_to_all | solution.py:139
  217.7 1.5 fusion.59
  219.9 1.6 collective-permute-start.60
  221.5 1.1 fusion.83
  223.3 4.1 %collective-permute-done.53 = bf16[64,2048]{1,0:T(8,128)(2,1)S(1)} collective-permute-done((bf16[64,2048]{1,0:T(8,128)(2,1)S(1)}, bf16[64,2048]{1,0:T(8,128)(2,1)S(1)}, u32[]{:S(2)}, u32[]{:S(2)}) %collective-permute-start.53) | collective-permute-done | bytes 262176 | tf_op jit(solution)/shard_map/ppermute | solution.py:56
  228.3 1.2 collective-permute-start.28
  229.5 1.6 fusion.62
  231.7 2.8 collective-permute-done.21
  234.5 1.2 collective-permute-start.54
  237.6 8.8 %collective-permute-done.54 = bf16[128,2048]{1,0:T(8,128)(2,1)S(1)} collective-permute-done((bf16[128,2048]{1,0:T(8,128)(2,1)S(1)}, bf16[128,2048]{1,0:T(8,128)(2,1)S(1)}, u32[]{:S(2)}, u32[]{:S(2)}) %collective-permute-start.54) | collective-permute-done | bytes 524320 | tf_op jit(solution)/shard_map/ppermute | solution.py:56
  246.3 1.6 collective-permute-start.22
  249.9 8.5 %collective-permute-done.22 = bf16[128,2048]{1,0:T(8,128)(2,1)S(1)} collective-permute-done((bf16[128,2048]{1,0:T(8,128)(2,1)S(1)}, bf16[128,2048]{1,0:T(8,128)(2,1)S(1)}, u32[]{:S(2)}, u32[]{:S(2)}) %collective-permute-start.22) | collective-permute-done | bytes 524320 | tf_op jit(solution)/shard_map/ppermute | solution.py:56
  258.4 1.6 collective-permute-start.55
  262.0 8.5 %collective-permute-done.55 = bf16[128,2048]{1,0:T(8,128)(2,1)S(1)} collective-permute-done((bf16[128,2048]{1,0:T(8,128)(2,1)S(1)}, bf16[128,2048]{1,0:T(8,128)(2,1)S(1)}, u32[]{:S(2)}, u32[]{:S(2)}) %collective-permute-start.55) | collective-permute-done | bytes 524320 | tf_op jit(solution)/shard_map/ppermute | solution.py:56
  270.5 1.6 collective-permute-start.23
  273.6 1.6 collective-permute-start.56
  275.2 8.1 %collective-permute-done.23 = bf16[128,2048]{1,0:T(8,128)(2,1)S(1)} collective-permute-done((bf16[128,2048]{1,0:T(8,128)(2,1)S(1)}, bf16[128,2048]{1,0:T(8,128)(2,1)S(1)}, u32[]{:S(2)}, u32[]{:S(2)}) %collective-permute-start.23) | collective-permute-done | bytes 524320 | tf_op jit(solution)/shard_map/ppermute | solution.py:56
  283.3 1.7 collective-permute-start.63
  285.9 1.7 collective-permute-start.31
  287.6 6.9 %collective-permute-done.56 = bf16[128,2048]{1,0:T(8,128)(2,1)S(1)} collective-permute-done((bf16[128,2048]{1,0:T(8,128)(2,1)S(1)}, bf16[128,2048]{1,0:T(8,128)(2,1)S(1)}, u32[]{:S(2)}, u32[]{:S(2)}) %collective-permute-start.56) | collective-permute-done | bytes 524320 | tf_op jit(solution)/shard_map/ppermute | solution.py:56
  294.5 3.6 %collective-permute-done.63 = bf16[128,2048]{1,0:T(8,128)(2,1)S(1)} collective-permute-done((bf16[128,2048]{1,0:T(8,128)(2,1)S(1)}, bf16[128,2048]{1,0:T(8,128)(2,1)S(1)}, u32[]{:S(2)}, u32[]{:S(2)}) %collective-permute-start.63) | collective-permute-done | bytes 524320 | tf_op jit(solution)/shard_map/ppermute | solution.py:53
  299.3 3.2 %collective-permute-done.24 = bf16[128,2048]{1,0:T(8,128)(2,1)S(1)} collective-permute-done((bf16[128,2048]{1,0:T(8,128)(2,1)S(1)}, bf16[128,2048]{1,0:T(8,128)(2,1)S(1)}, u32[]{:S(2)}, u32[]{:S(2)}) %collective-permute-start.24) | collective-permute-done | bytes 524320 | tf_op jit(solution)/shard_map/ppermute | solution.py:56
  302.5 1.4 collective-permute-done.31
  303.9 1.1 fusion.96
  (232 shorter events, 43.5 us)
Async XLA Ops:
  0.6 21.8 %collective-permute-start.3 = (bf16[128,2048]{1,0:T(8,128)(2,1)}, bf16[128,2048]{1,0:T(8,128)(2,1)S(1)}, u32[]{:S(2)}, u32[]{:S(2)}) collective-permute-start(bf16[128,2048]{1,0:T(8,128)(2,1)} %param.9), channel_id=1, source_target_pairs={{0,2},{1,3},{4,0},{5,1},{8,4},{9,5},{12,8},{13,9},{14,12},{15,13},... | collective-permute-start | bytes 1572872 | tf_op jit(solution)/shard_map/ppermute | solution.py:56
  3.6 18.3 %collective-permute-start.1 = (bf16[128,2048]{1,0:T(8,128)(2,1)}, bf16[128,2048]{1,0:T(8,128)(2,1)S(1)}, u32[]{:S(2)}, u32[]{:S(2)}) collective-permute-start(bf16[128,2048]{1,0:T(8,128)(2,1)} %param.9), channel_id=1, source_target_pairs={{0,4},{1,5},{4,8},{5,9},{8,12},{9,13},{12,14},{13,15},{14,10},{15,... | collective-permute-start | bytes 1572872 | tf_op jit(solution)/shard_map/ppermute | solution.py:53
  3.8 20.5 %collective-permute-start = (bf16[128,2048]{1,0:T(8,128)(2,1)}, bf16[128,2048]{1,0:T(8,128)(2,1)S(1)}, u32[]{:S(2)}, u32[]{:S(2)}) collective-permute-start(bf16[128,2048]{1,0:T(8,128)(2,1)} %param.9), channel_id=1, source_target_pairs={{0,1},{1,0},{2,3},{3,2},{4,5},{5,4},{6,7},{7,6},{8,9},{9,8},{10,11... | collective-permute-start | bytes 1572872 | tf_op jit(solution)/shard_map/ppermute | solution.py:59
  5.1 15.4 %all-to-all-start = ((f32[16,2,128]{2,1,0:T(2,128)}), f32[16,2,128]{2,1,0:T(2,128)S(1)}, u32[]{:S(2)}, u32[]{:S(2)}) async-start(f32[16,2,128]{2,1,0:T(2,128)} %bitcast.1), calls=%async_computation | async-start | bytes 32768 | tf_op jit(solution)/shard_map/all_to_all | solution.py:74
  22.0 13.6 %collective-permute-start.5 = (bf16[128,2048]{1,0:T(8,128)(2,1)S(1)}, bf16[128,2048]{1,0:T(8,128)(2,1)S(1)}, u32[]{:S(2)}, u32[]{:S(2)}) collective-permute-start(bf16[128,2048]{1,0:T(8,128)(2,1)S(1)} %collective-permute-done.1), channel_id=1, source_target_pairs={{0,4},{1,5},{4,8},{5,9},{8,12},{9,13},{12,14},{13,15},{14,10},{15,... | collective-permute-start | bytes 1572872 | tf_op jit(solution)/shard_map/ppermute | solution.py:53
  22.5 15.9 %collective-permute-start.2 = (bf16[128,2048]{1,0:T(8,128)(2,1)S(1)}, bf16[128,2048]{1,0:T(8,128)(2,1)S(1)}, u32[]{:S(2)}, u32[]{:S(2)}) collective-permute-start(bf16[128,2048]{1,0:T(8,128)(2,1)S(1)} %collective-permute-done.1), channel_id=1, source_target_pairs={{0,1},{1,0},{2,3},{3,2},{4,5},{5,4},{6,7},{7,6},{8,9},{9,8},{10,11... | collective-permute-start | bytes 1572872 | tf_op jit(solution)/shard_map/ppermute | solution.py:59
  22.5 14.3 %collective-permute-start.7 = (bf16[128,2048]{1,0:T(8,128)(2,1)S(1)}, bf16[128,2048]{1,0:T(8,128)(2,1)S(1)}, u32[]{:S(2)}, u32[]{:S(2)}) collective-permute-start(bf16[128,2048]{1,0:T(8,128)(2,1)S(1)} %collective-permute-done.3), channel_id=1, source_target_pairs={{0,2},{1,3},{4,0},{5,1},{8,4},{9,5},{12,8},{13,9},{14,12},{15,13},... | collective-permute-start | bytes 1572872 | tf_op jit(solution)/shard_map/ppermute | solution.py:56
  24.0 14.3 %collective-permute-start.4 = (bf16[128,2048]{1,0:T(8,128)(2,1)S(1)}, bf16[128,2048]{1,0:T(8,128)(2,1)S(1)}, u32[]{:S(2)}, u32[]{:S(2)}) collective-permute-start(bf16[128,2048]{1,0:T(8,128)(2,1)S(1)} %collective-permute-done.3), channel_id=1, source_target_pairs={{0,1},{1,0},{2,3},{3,2},{4,5},{5,4},{6,7},{7,6},{8,9},{9,8},{10,11... | collective-permute-start | bytes 1572872 | tf_op jit(solution)/shard_map/ppermute | solution.py:59
  35.6 15.2 %collective-permute-start.9 = (bf16[128,2048]{1,0:T(8,128)(2,1)S(1)}, bf16[128,2048]{1,0:T(8,128)(2,1)S(1)}, u32[]{:S(2)}, u32[]{:S(2)}) collective-permute-start(bf16[128,2048]{1,0:T(8,128)(2,1)S(1)} %collective-permute-done.5), channel_id=1, source_target_pairs={{0,4},{1,5},{4,8},{5,9},{8,12},{9,13},{12,14},{13,15},{14,10},{15,... | collective-permute-start | bytes 1572872 | tf_op jit(solution)/shard_map/ppermute | solution.py:53
  36.4 15.3 %collective-permute-start.6 = (bf16[128,2048]{1,0:T(8,128)(2,1)S(1)}, bf16[128,2048]{1,0:T(8,128)(2,1)S(1)}, u32[]{:S(2)}, u32[]{:S(2)}) collective-permute-start(bf16[128,2048]{1,0:T(8,128)(2,1)S(1)} %collective-permute-done.5), channel_id=1, source_target_pairs={{0,1},{1,0},{2,3},{3,2},{4,5},{5,4},{6,7},{7,6},{8,9},{9,8},{10,11... | collective-permute-start | bytes 1572872 | tf_op jit(solution)/shard_map/ppermute | solution.py:59
  36.8 13.9 %collective-permute-start.11 = (bf16[128,2048]{1,0:T(8,128)(2,1)S(1)}, bf16[128,2048]{1,0:T(8,128)(2,1)S(1)}, u32[]{:S(2)}, u32[]{:S(2)}) collective-permute-start(bf16[128,2048]{1,0:T(8,128)(2,1)S(1)} %collective-permute-done.7), channel_id=1, source_target_pairs={{0,2},{1,3},{4,0},{5,1},{8,4},{9,5},{12,8},{13,9},{14,12},{15,13},... | collective-permute-start | bytes 1572872 | tf_op jit(solution)/shard_map/ppermute | solution.py:56
  38.4 13.3 %collective-permute-start.8 = (bf16[128,2048]{1,0:T(8,128)(2,1)S(1)}, bf16[128,2048]{1,0:T(8,128)(2,1)S(1)}, u32[]{:S(2)}, u32[]{:S(2)}) collective-permute-start(bf16[128,2048]{1,0:T(8,128)(2,1)S(1)} %collective-permute-done.7), channel_id=1, source_target_pairs={{0,1},{1,0},{2,3},{3,2},{4,5},{5,4},{6,7},{7,6},{8,9},{9,8},{10,11... | collective-permute-start | bytes 1572872 | tf_op jit(solution)/shard_map/ppermute | solution.py:59
  50.8 22.0 %collective-permute-start.33 = (bf16[128,2048]{1,0:T(8,128)(2,1)S(1)}, bf16[128,2048]{1,0:T(8,128)(2,1)S(1)}, u32[]{:S(2)}, u32[]{:S(2)}) collective-permute-start(bf16[128,2048]{1,0:T(8,128)(2,1)S(1)} %copy-done.13), channel_id=1, source_target_pairs={{0,4},{1,5},{4,8},{5,9},{8,12},{9,13},{12,14},{13,15},{14,10},{15,... | collective-permute-start | bytes 1572872 | tf_op jit(solution)/shard_map/ppermute | solution.py:53
  51.4 18.1 %collective-permute-start.13 = (bf16[64,2048]{1,0:T(8,128)(2,1)S(1)}, bf16[64,2048]{1,0:T(8,128)(2,1)S(1)}, u32[]{:S(2)}, u32[]{:S(2)}) collective-permute-start(bf16[64,2048]{1,0:T(8,128)(2,1)S(1)} %slice.280), channel_id=1, source_target_pairs={{0,4},{1,5},{4,8},{5,9},{8,12},{9,13},{12,14},{13,15},{14,10},{15,... | collective-permute-start | bytes 786440 | tf_op jit(solution)/shard_map/ppermute | solution.py:53
  52.3 18.0 %collective-permute-start.14 = (bf16[64,2048]{1,0:T(8,128)(2,1)S(1)}, bf16[64,2048]{1,0:T(8,128)(2,1)S(1)}, u32[]{:S(2)}, u32[]{:S(2)}) collective-permute-start(bf16[64,2048]{1,0:T(8,128)(2,1)S(1)} %slice.281), channel_id=1, source_target_pairs={{0,2},{1,3},{4,0},{5,1},{8,4},{9,5},{12,8},{13,9},{14,12},{15,13},... | collective-permute-start | bytes 786440 | tf_op jit(solution)/shard_map/ppermute | solution.py:56
  54.1 16.3 %collective-permute-start.10 = (bf16[128,2048]{1,0:T(8,128)(2,1)S(1)}, bf16[128,2048]{1,0:T(8,128)(2,1)S(1)}, u32[]{:S(2)}, u32[]{:S(2)}) collective-permute-start(bf16[128,2048]{1,0:T(8,128)(2,1)S(1)} %collective-permute-done.9), channel_id=1, source_target_pairs={{0,1},{1,0},{2,3},{3,2},{4,5},{5,4},{6,7},{7,6},{8,9},{9,8},{10,11... | collective-permute-start | bytes 1572872 | tf_op jit(solution)/shard_map/ppermute | solution.py:59
  54.1 16.8 %collective-permute-start.12 = (bf16[128,2048]{1,0:T(8,128)(2,1)S(1)}, bf16[128,2048]{1,0:T(8,128)(2,1)S(1)}, u32[]{:S(2)}, u32[]{:S(2)}) collective-permute-start(bf16[128,2048]{1,0:T(8,128)(2,1)S(1)} %collective-permute-done.11), channel_id=1, source_target_pairs={{0,1},{1,0},{2,3},{3,2},{4,5},{5,4},{6,7},{7,6},{8,9},{9,8},{10,11... | collective-permute-start | bytes 1572872 | tf_op jit(solution)/shard_map/ppermute | solution.py:59
  69.5 12.2 %collective-permute-start.35 = (bf16[128,2048]{1,0:T(8,128)(2,1)S(1)}, bf16[128,2048]{1,0:T(8,128)(2,1)S(1)}, u32[]{:S(2)}, u32[]{:S(2)}) collective-permute-start(bf16[128,2048]{1,0:T(8,128)(2,1)S(1)} %copy-done.13), channel_id=1, source_target_pairs={{0,2},{1,3},{4,0},{5,1},{8,4},{9,5},{12,8},{13,9},{14,12},{15,13},... | collective-permute-start | bytes 1572872 | tf_op jit(solution)/shard_map/ppermute | solution.py:56
  70.4 12.0 %collective-permute-start.15 = (bf16[128,2048]{1,0:T(8,128)(2,1)S(1)}, bf16[128,2048]{1,0:T(8,128)(2,1)S(1)}, u32[]{:S(2)}, u32[]{:S(2)}) collective-permute-start(bf16[128,2048]{1,0:T(8,128)(2,1)S(1)} %constant_dynamic-update-slice_fusion), channel_id=1, source_target_pairs={{0,1},{1,0},{2,3},{3,2},{4,5},{5,4},{6,7},{7,6},{8,9},{9,8},{10,11... | collective-permute-start | bytes 1572872 | tf_op jit(solution)/shard_map/ppermute | solution.py:59
  72.8 23.4 %collective-permute-start.34 = (bf16[128,2048]{1,0:T(8,128)(2,1)S(1)}, bf16[128,2048]{1,0:T(8,128)(2,1)S(1)}, u32[]{:S(2)}, u32[]{:S(2)}) collective-permute-start(bf16[128,2048]{1,0:T(8,128)(2,1)S(1)} %collective-permute-done.33), channel_id=1, source_target_pairs={{0,1},{1,0},{2,3},{3,2},{4,5},{5,4},{6,7},{7,6},{8,9},{9,8},{10,11... | collective-permute-start | bytes 1572872 | tf_op jit(solution)/shard_map/ppermute | solution.py:59
  73.0 20.4 %collective-permute-start.37 = (bf16[128,2048]{1,0:T(8,128)(2,1)S(1)}, bf16[128,2048]{1,0:T(8,128)(2,1)S(1)}, u32[]{:S(2)}, u32[]{:S(2)}) collective-permute-start(bf16[128,2048]{1,0:T(8,128)(2,1)S(1)} %collective-permute-done.33), channel_id=1, source_target_pairs={{0,4},{1,5},{4,8},{5,9},{8,12},{9,13},{12,14},{13,15},{14,10},{15,... | collective-permute-start | bytes 1572872 | tf_op jit(solution)/shard_map/ppermute | solution.py:53
  81.7 14.5 %collective-permute-start.36 = (bf16[128,2048]{1,0:T(8,128)(2,1)S(1)}, bf16[128,2048]{1,0:T(8,128)(2,1)S(1)}, u32[]{:S(2)}, u32[]{:S(2)}) collective-permute-start(bf16[128,2048]{1,0:T(8,128)(2,1)S(1)} %collective-permute-done.35), channel_id=1, source_target_pairs={{0,1},{1,0},{2,3},{3,2},{4,5},{5,4},{6,7},{7,6},{8,9},{9,8},{10,11... | collective-permute-start | bytes 1572872 | tf_op jit(solution)/shard_map/ppermute | solution.py:59
  81.7 14.5 %collective-permute-start.39 = (bf16[128,2048]{1,0:T(8,128)(2,1)S(1)}, bf16[128,2048]{1,0:T(8,128)(2,1)S(1)}, u32[]{:S(2)}, u32[]{:S(2)}) collective-permute-start(bf16[128,2048]{1,0:T(8,128)(2,1)S(1)} %collective-permute-done.35), channel_id=1, source_target_pairs={{0,2},{1,3},{4,0},{5,1},{8,4},{9,5},{12,8},{13,9},{14,12},{15,13},... | collective-permute-start | bytes 1572872 | tf_op jit(solution)/shard_map/ppermute | solution.py:56
  93.4 16.1 %collective-permute-start.38 = (bf16[128,2048]{1,0:T(8,128)(2,1)S(1)}, bf16[128,2048]{1,0:T(8,128)(2,1)S(1)}, u32[]{:S(2)}, u32[]{:S(2)}) collective-permute-start(bf16[128,2048]{1,0:T(8,128)(2,1)S(1)} %collective-permute-done.37), channel_id=1, source_target_pairs={{0,1},{1,0},{2,3},{3,2},{4,5},{5,4},{6,7},{7,6},{8,9},{9,8},{10,11... | collective-permute-start | bytes 1572872 | tf_op jit(solution)/shard_map/ppermute | solution.py:59
  93.6 14.1 %collective-permute-start.41 = (bf16[128,2048]{1,0:T(8,128)(2,1)S(1)}, bf16[128,2048]{1,0:T(8,128)(2,1)S(1)}, u32[]{:S(2)}, u32[]{:S(2)}) collective-permute-start(bf16[128,2048]{1,0:T(8,128)(2,1)S(1)} %collective-permute-done.37), channel_id=1, source_target_pairs={{0,4},{1,5},{4,8},{5,9},{8,12},{9,13},{12,14},{13,15},{14,10},{15,... | collective-permute-start | bytes 1572872 | tf_op jit(solution)/shard_map/ppermute | solution.py:53
  96.2 13.2 %collective-permute-start.40 = (bf16[128,2048]{1,0:T(8,128)(2,1)S(1)}, bf16[128,2048]{1,0:T(8,128)(2,1)S(1)}, u32[]{:S(2)}, u32[]{:S(2)}) collective-permute-start(bf16[128,2048]{1,0:T(8,128)(2,1)S(1)} %collective-permute-done.39), channel_id=1, source_target_pairs={{0,1},{1,0},{2,3},{3,2},{4,5},{5,4},{6,7},{7,6},{8,9},{9,8},{10,11... | collective-permute-start | bytes 1572872 | tf_op jit(solution)/shard_map/ppermute | solution.py:59
  96.8 14.4 %collective-permute-start.43 = (bf16[128,2048]{1,0:T(8,128)(2,1)S(1)}, bf16[128,2048]{1,0:T(8,128)(2,1)S(1)}, u32[]{:S(2)}, u32[]{:S(2)}) collective-permute-start(bf16[128,2048]{1,0:T(8,128)(2,1)S(1)} %collective-permute-done.39), channel_id=1, source_target_pairs={{0,2},{1,3},{4,0},{5,1},{8,4},{9,5},{12,8},{13,9},{14,12},{15,13},... | collective-permute-start | bytes 1572872 | tf_op jit(solution)/shard_map/ppermute | solution.py:56
  107.7 7.7 %collective-permute-start.45 = (bf16[64,2048]{1,0:T(8,128)(2,1)S(1)}, bf16[64,2048]{1,0:T(8,128)(2,1)S(1)}, u32[]{:S(2)}, u32[]{:S(2)}) collective-permute-start(bf16[64,2048]{1,0:T(8,128)(2,1)S(1)} %slice.305), channel_id=1, source_target_pairs={{0,4},{1,5},{4,8},{5,9},{8,12},{9,13},{12,14},{13,15},{14,10},{15,... | collective-permute-start | bytes 786440 | tf_op jit(solution)/shard_map/ppermute | solution.py:53
  111.2 8.4 %collective-permute-start.46 = (bf16[64,2048]{1,0:T(8,128)(2,1)S(1)}, bf16[64,2048]{1,0:T(8,128)(2,1)S(1)}, u32[]{:S(2)}, u32[]{:S(2)}) collective-permute-start(bf16[64,2048]{1,0:T(8,128)(2,1)S(1)} %slice.306), channel_id=1, source_target_pairs={{0,2},{1,3},{4,0},{5,1},{8,4},{9,5},{12,8},{13,9},{14,12},{15,13},... | collective-permute-start | bytes 786440 | tf_op jit(solution)/shard_map/ppermute | solution.py:56
  112.1 7.6 %collective-permute-start.42 = (bf16[128,2048]{1,0:T(8,128)(2,1)S(1)}, bf16[128,2048]{1,0:T(8,128)(2,1)S(1)}, u32[]{:S(2)}, u32[]{:S(2)}) collective-permute-start(bf16[128,2048]{1,0:T(8,128)(2,1)S(1)} %collective-permute-done.41), channel_id=1, source_target_pairs={{0,1},{1,0},{2,3},{3,2},{4,5},{5,4},{6,7},{7,6},{8,9},{9,8},{10,11... | collective-permute-start | bytes 1572872 | tf_op jit(solution)/shard_map/ppermute | solution.py:59
  112.1 7.7 %collective-permute-start.44 = (bf16[128,2048]{1,0:T(8,128)(2,1)S(1)}, bf16[128,2048]{1,0:T(8,128)(2,1)S(1)}, u32[]{:S(2)}, u32[]{:S(2)}) collective-permute-start(bf16[128,2048]{1,0:T(8,128)(2,1)S(1)} %collective-permute-done.43), channel_id=1, source_target_pairs={{0,1},{1,0},{2,3},{3,2},{4,5},{5,4},{6,7},{7,6},{8,9},{9,8},{10,11... | collective-permute-start | bytes 1572872 | tf_op jit(solution)/shard_map/ppermute | solution.py:59
  175.9 41.8 %collective-permute-start.52 = (bf16[128,2048]{1,0:T(8,128)(2,1)}, bf16[128,2048]{1,0:T(8,128)(2,1)}, u32[]{:S(2)}, u32[]{:S(2)}) collective-permute-start(bf16[128,2048]{1,0:T(8,128)(2,1)} %fusion.113), channel_id=1, source_target_pairs={{0,1},{1,0},{2,3},{3,2},{4,5},{5,4},{6,7},{7,6},{8,9},{9,8},{10,11... | collective-permute-start | bytes 1572872 | tf_op jit(solution)/shard_map/ppermute | solution.py:59
  180.0 42.8 %collective-permute-start.51 = (bf16[128,2048]{1,0:T(8,128)(2,1)}, bf16[128,2048]{1,0:T(8,128)(2,1)}, u32[]{:S(2)}, u32[]{:S(2)}) collective-permute-start(bf16[128,2048]{1,0:T(8,128)(2,1)} %get-tuple-element.35), channel_id=1, source_target_pairs={{0,1},{1,0},{2,3},{3,2},{4,5},{5,4},{6,7},{7,6},{8,9},{9,8},{10,11... | collective-permute-start | bytes 1572872 | tf_op jit(solution)/shard_map/ppermute | solution.py:59
  180.3 42.5 %collective-permute-start.59 = (bf16[128,2048]{1,0:T(8,128)(2,1)}, bf16[128,2048]{1,0:T(8,128)(2,1)}, u32[]{:S(2)}, u32[]{:S(2)}) collective-permute-start(bf16[128,2048]{1,0:T(8,128)(2,1)} %get-tuple-element.36), channel_id=1, source_target_pairs={{0,1},{1,0},{2,3},{3,2},{4,5},{5,4},{6,7},{7,6},{8,9},{9,8},{10,11... | collective-permute-start | bytes 1572872 | tf_op jit(solution)/shard_map/ppermute | solution.py:59
  184.5 52.5 %collective-permute-start.50 = (bf16[128,2048]{1,0:T(8,128)(2,1)}, bf16[128,2048]{1,0:T(8,128)(2,1)S(1)}, u32[]{:S(2)}, u32[]{:S(2)}) collective-permute-start(bf16[128,2048]{1,0:T(8,128)(2,1)} %get-tuple-element.33), channel_id=1, source_target_pairs={{0,1},{1,0},{2,3},{3,2},{4,5},{5,4},{6,7},{7,6},{8,9},{9,8},{10,11... | collective-permute-start | bytes 1572872 | tf_op jit(solution)/shard_map/ppermute | solution.py:59
  192.2 27.8 %collective-permute-start.20 = (bf16[128,2048]{1,0:T(8,128)(2,1)}, bf16[128,2048]{1,0:T(8,128)(2,1)}, u32[]{:S(2)}, u32[]{:S(2)}) collective-permute-start(bf16[128,2048]{1,0:T(8,128)(2,1)} %fusion.111), channel_id=1, source_target_pairs={{0,1},{1,0},{2,3},{3,2},{4,5},{5,4},{6,7},{7,6},{8,9},{9,8},{10,11... | collective-permute-start | bytes 1572872 | tf_op jit(solution)/shard_map/ppermute | solution.py:59
  207.1 10.0 %all-to-all-start.1 = ((f32[16,2,128]{2,1,0:T(2,128)}), f32[16,2,128]{2,1,0:T(2,128)S(1)}, u32[]{:S(2)}, u32[]{:S(2)}) async-start(f32[16,2,128]{2,1,0:T(2,128)} %gather_fusion.1), calls=%async_computation.1 | async-start | bytes 32768 | tf_op jit(solution)/shard_map/all_to_all | solution.py:139
  219.2 8.2 %collective-permute-start.53 = (bf16[64,2048]{1,0:T(8,128)(2,1)S(1)}, bf16[64,2048]{1,0:T(8,128)(2,1)S(1)}, u32[]{:S(2)}, u32[]{:S(2)}) collective-permute-start(bf16[64,2048]{1,0:T(8,128)(2,1)S(1)} %get-tuple-element.43), channel_id=1, source_target_pairs={{0,2},{1,3},{4,0},{5,1},{8,4},{9,5},{12,8},{13,9},{14,12},{15,13},... | collective-permute-start | bytes 786440 | tf_op jit(solution)/shard_map/ppermute | solution.py:56
  219.9 8.3 %collective-permute-start.60 = (bf16[64,2048]{1,0:T(8,128)(2,1)S(1)}, bf16[64,2048]{1,0:T(8,128)(2,1)S(1)}, u32[]{:S(2)}, u32[]{:S(2)}) collective-permute-start(bf16[64,2048]{1,0:T(8,128)(2,1)S(1)} %get-tuple-element.44), channel_id=1, source_target_pairs={{0,4},{1,5},{4,8},{5,9},{8,12},{9,13},{12,14},{13,15},{14,10},{15,... | collective-permute-start | bytes 786440 | tf_op jit(solution)/shard_map/ppermute | solution.py:53
  222.8 8.4 %collective-permute-start.19 = (bf16[128,2048]{1,0:T(8,128)(2,1)}, bf16[128,2048]{1,0:T(8,128)(2,1)S(1)}, u32[]{:S(2)}, u32[]{:S(2)}) collective-permute-start(bf16[128,2048]{1,0:T(8,128)(2,1)} %get-tuple-element.41), channel_id=1, source_target_pairs={{0,1},{1,0},{2,3},{3,2},{4,5},{5,4},{6,7},{7,6},{8,9},{9,8},{10,11... | collective-permute-start | bytes 1572872 | tf_op jit(solution)/shard_map/ppermute | solution.py:59
  222.8 8.4 %collective-permute-start.27 = (bf16[128,2048]{1,0:T(8,128)(2,1)}, bf16[128,2048]{1,0:T(8,128)(2,1)S(1)}, u32[]{:S(2)}, u32[]{:S(2)}) collective-permute-start(bf16[128,2048]{1,0:T(8,128)(2,1)} %get-tuple-element.42), channel_id=1, source_target_pairs={{0,1},{1,0},{2,3},{3,2},{4,5},{5,4},{6,7},{7,6},{8,9},{9,8},{10,11... | collective-permute-start | bytes 1572872 | tf_op jit(solution)/shard_map/ppermute | solution.py:59
  227.5 7.1 %collective-permute-start.21 = (bf16[64,2048]{1,0:T(8,128)(2,1)S(1)}, bf16[64,2048]{1,0:T(8,128)(2,1)S(1)}, u32[]{:S(2)}, u32[]{:S(2)}) collective-permute-start(bf16[64,2048]{1,0:T(8,128)(2,1)S(1)} %get-tuple-element.45), channel_id=1, source_target_pairs={{0,2},{1,3},{4,0},{5,1},{8,4},{9,5},{12,8},{13,9},{14,12},{15,13},... | collective-permute-start | bytes 786440 | tf_op jit(solution)/shard_map/ppermute | solution.py:56
  228.3 7.5 %collective-permute-start.28 = (bf16[64,2048]{1,0:T(8,128)(2,1)S(1)}, bf16[64,2048]{1,0:T(8,128)(2,1)S(1)}, u32[]{:S(2)}, u32[]{:S(2)}) collective-permute-start(bf16[64,2048]{1,0:T(8,128)(2,1)S(1)} %get-tuple-element.46), channel_id=1, source_target_pairs={{0,4},{1,5},{4,8},{5,9},{8,12},{9,13},{12,14},{13,15},{14,10},{15,... | collective-permute-start | bytes 786440 | tf_op jit(solution)/shard_map/ppermute | solution.py:53
  231.1 5.9 %collective-permute-start.58 = (bf16[128,2048]{1,0:T(8,128)(2,1)}, bf16[128,2048]{1,0:T(8,128)(2,1)S(1)}, u32[]{:S(2)}, u32[]{:S(2)}) collective-permute-start(bf16[128,2048]{1,0:T(8,128)(2,1)} %get-tuple-element.34), channel_id=1, source_target_pairs={{0,1},{1,0},{2,3},{3,2},{4,5},{5,4},{6,7},{7,6},{8,9},{9,8},{10,11... | collective-permute-start | bytes 1572872 | tf_op jit(solution)/shard_map/ppermute | solution.py:59
  231.2 29.7 %collective-permute-start.49 = (bf16[128,2048]{1,0:T(8,128)(2,1)S(1)}, bf16[128,2048]{1,0:T(8,128)(2,1)S(1)}, u32[]{:S(2)}, u32[]{:S(2)}) collective-permute-start(bf16[128,2048]{1,0:T(8,128)(2,1)S(1)} %copy-done.16), channel_id=1, source_target_pairs={{0,1},{1,0},{2,3},{3,2},{4,5},{5,4},{6,7},{7,6},{8,9},{9,8},{10,11... | collective-permute-start | bytes 1572872 | tf_op jit(solution)/shard_map/ppermute | solution.py:59
  234.5 11.8 %collective-permute-start.54 = (bf16[128,2048]{1,0:T(8,128)(2,1)S(1)}, bf16[128,2048]{1,0:T(8,128)(2,1)S(1)}, u32[]{:S(2)}, u32[]{:S(2)}) collective-permute-start(bf16[128,2048]{1,0:T(8,128)(2,1)S(1)} %get-tuple-element.23), channel_id=1, source_target_pairs={{0,2},{1,3},{4,0},{5,1},{8,4},{9,5},{12,8},{13,9},{14,12},{15,13},... | collective-permute-start | bytes 1572872 | tf_op jit(solution)/shard_map/ppermute | solution.py:56
  235.8 12.2 %collective-permute-start.61 = (bf16[128,2048]{1,0:T(8,128)(2,1)S(1)}, bf16[128,2048]{1,0:T(8,128)(2,1)S(1)}, u32[]{:S(2)}, u32[]{:S(2)}) collective-permute-start(bf16[128,2048]{1,0:T(8,128)(2,1)S(1)} %get-tuple-element.24), channel_id=1, source_target_pairs={{0,4},{1,5},{4,8},{5,9},{8,12},{9,13},{12,14},{13,15},{14,10},{15,... | collective-permute-start | bytes 1572872 | tf_op jit(solution)/shard_map/ppermute | solution.py:53
  237.0 11.9 %collective-permute-start.18 = (bf16[128,2048]{1,0:T(8,128)(2,1)}, bf16[128,2048]{1,0:T(8,128)(2,1)S(1)}, u32[]{:S(2)}, u32[]{:S(2)}) collective-permute-start(bf16[128,2048]{1,0:T(8,128)(2,1)} %get-tuple-element.39), channel_id=1, source_target_pairs={{0,1},{1,0},{2,3},{3,2},{4,5},{5,4},{6,7},{7,6},{8,9},{9,8},{10,11... | collective-permute-start | bytes 1572872 | tf_op jit(solution)/shard_map/ppermute | solution.py:59
  237.1 12.3 %collective-permute-start.26 = (bf16[128,2048]{1,0:T(8,128)(2,1)S(1)}, bf16[128,2048]{1,0:T(8,128)(2,1)S(1)}, u32[]{:S(2)}, u32[]{:S(2)}) collective-permute-start(bf16[128,2048]{1,0:T(8,128)(2,1)S(1)} %copy-done.19), channel_id=1, source_target_pairs={{0,1},{1,0},{2,3},{3,2},{4,5},{5,4},{6,7},{7,6},{8,9},{9,8},{10,11... | collective-permute-start | bytes 1572872 | tf_op jit(solution)/shard_map/ppermute | solution.py:59
  246.3 12.1 %collective-permute-start.22 = (bf16[128,2048]{1,0:T(8,128)(2,1)S(1)}, bf16[128,2048]{1,0:T(8,128)(2,1)S(1)}, u32[]{:S(2)}, u32[]{:S(2)}) collective-permute-start(bf16[128,2048]{1,0:T(8,128)(2,1)S(1)} %get-tuple-element.29), channel_id=1, source_target_pairs={{0,2},{1,3},{4,0},{5,1},{8,4},{9,5},{12,8},{13,9},{14,12},{15,13},... | collective-permute-start | bytes 1572872 | tf_op jit(solution)/shard_map/ppermute | solution.py:56
  248.0 12.1 %collective-permute-start.29 = (bf16[128,2048]{1,0:T(8,128)(2,1)S(1)}, bf16[128,2048]{1,0:T(8,128)(2,1)S(1)}, u32[]{:S(2)}, u32[]{:S(2)}) collective-permute-start(bf16[128,2048]{1,0:T(8,128)(2,1)S(1)} %get-tuple-element.30), channel_id=1, source_target_pairs={{0,4},{1,5},{4,8},{5,9},{8,12},{9,13},{12,14},{13,15},{14,10},{15,... | collective-permute-start | bytes 1572872 | tf_op jit(solution)/shard_map/ppermute | solution.py:53
  249.4 12.1 %collective-permute-start.57 = (bf16[128,2048]{1,0:T(8,128)(2,1)S(1)}, bf16[128,2048]{1,0:T(8,128)(2,1)S(1)}, u32[]{:S(2)}, u32[]{:S(2)}) collective-permute-start(bf16[128,2048]{1,0:T(8,128)(2,1)S(1)} %copy-done.15), channel_id=1, source_target_pairs={{0,1},{1,0},{2,3},{3,2},{4,5},{5,4},{6,7},{7,6},{8,9},{9,8},{10,11... | collective-permute-start | bytes 1572872 | tf_op jit(solution)/shard_map/ppermute | solution.py:59
  249.4 36.5 %collective-permute-start.48 = (bf16[128,2048]{1,0:T(8,128)(2,1)S(1)}, bf16[128,2048]{1,0:T(8,128)(2,1)S(1)}, u32[]{:S(2)}, u32[]{:S(2)}) collective-permute-start(bf16[128,2048]{1,0:T(8,128)(2,1)S(1)} %fusion.112), channel_id=1, source_target_pairs={{0,1},{1,0},{2,3},{3,2},{4,5},{5,4},{6,7},{7,6},{8,9},{9,8},{10,11... | collective-permute-start | bytes 1572872 | tf_op jit(solution)/shard_map/ppermute | solution.py:59
  258.4 12.1 %collective-permute-start.55 = (bf16[128,2048]{1,0:T(8,128)(2,1)S(1)}, bf16[128,2048]{1,0:T(8,128)(2,1)S(1)}, u32[]{:S(2)}, u32[]{:S(2)}) collective-permute-start(bf16[128,2048]{1,0:T(8,128)(2,1)S(1)} %get-tuple-element.21), channel_id=1, source_target_pairs={{0,2},{1,3},{4,0},{5,1},{8,4},{9,5},{12,8},{13,9},{14,12},{15,13},... | collective-permute-start | bytes 1572872 | tf_op jit(solution)/shard_map/ppermute | solution.py:56
  260.0 12.1 %collective-permute-start.62 = (bf16[128,2048]{1,0:T(8,128)(2,1)S(1)}, bf16[128,2048]{1,0:T(8,128)(2,1)S(1)}, u32[]{:S(2)}, u32[]{:S(2)}) collective-permute-start(bf16[128,2048]{1,0:T(8,128)(2,1)S(1)} %get-tuple-element.22), channel_id=1, source_target_pairs={{0,4},{1,5},{4,8},{5,9},{8,12},{9,13},{12,14},{13,15},{14,10},{15,... | collective-permute-start | bytes 1572872 | tf_op jit(solution)/shard_map/ppermute | solution.py:53
  261.5 11.6 %collective-permute-start.17 = (bf16[128,2048]{1,0:T(8,128)(2,1)S(1)}, bf16[128,2048]{1,0:T(8,128)(2,1)S(1)}, u32[]{:S(2)}, u32[]{:S(2)}) collective-permute-start(bf16[128,2048]{1,0:T(8,128)(2,1)S(1)} %copy-done.18), channel_id=1, source_target_pairs={{0,1},{1,0},{2,3},{3,2},{4,5},{5,4},{6,7},{7,6},{8,9},{9,8},{10,11... | collective-permute-start | bytes 1572872 | tf_op jit(solution)/shard_map/ppermute | solution.py:59
  261.7 11.9 %collective-permute-start.25 = (bf16[128,2048]{1,0:T(8,128)(2,1)S(1)}, bf16[128,2048]{1,0:T(8,128)(2,1)S(1)}, u32[]{:S(2)}, u32[]{:S(2)}) collective-permute-start(bf16[128,2048]{1,0:T(8,128)(2,1)S(1)} %copy-done.17), channel_id=1, source_target_pairs={{0,1},{1,0},{2,3},{3,2},{4,5},{5,4},{6,7},{7,6},{8,9},{9,8},{10,11... | collective-permute-start | bytes 1572872 | tf_op jit(solution)/shard_map/ppermute | solution.py:59
  270.5 12.8 %collective-permute-start.23 = (bf16[128,2048]{1,0:T(8,128)(2,1)S(1)}, bf16[128,2048]{1,0:T(8,128)(2,1)S(1)}, u32[]{:S(2)}, u32[]{:S(2)}) collective-permute-start(bf16[128,2048]{1,0:T(8,128)(2,1)S(1)} %get-tuple-element.27), channel_id=1, source_target_pairs={{0,2},{1,3},{4,0},{5,1},{8,4},{9,5},{12,8},{13,9},{14,12},{15,13},... | collective-permute-start | bytes 1572872 | tf_op jit(solution)/shard_map/ppermute | solution.py:56
  272.1 12.9 %collective-permute-start.30 = (bf16[128,2048]{1,0:T(8,128)(2,1)S(1)}, bf16[128,2048]{1,0:T(8,128)(2,1)S(1)}, u32[]{:S(2)}, u32[]{:S(2)}) collective-permute-start(bf16[128,2048]{1,0:T(8,128)(2,1)S(1)} %get-tuple-element.28), channel_id=1, source_target_pairs={{0,4},{1,5},{4,8},{5,9},{8,12},{9,13},{12,14},{13,15},{14,10},{15,... | collective-permute-start | bytes 1572872 | tf_op jit(solution)/shard_map/ppermute | solution.py:53
  273.6 25.7 %collective-permute-start.16 = (bf16[128,2048]{1,0:T(8,128)(2,1)S(1)}, bf16[128,2048]{1,0:T(8,128)(2,1)S(1)}, u32[]{:S(2)}, u32[]{:S(2)}) collective-permute-start(bf16[128,2048]{1,0:T(8,128)(2,1)S(1)} %copy-done.14), channel_id=1, source_target_pairs={{0,1},{1,0},{2,3},{3,2},{4,5},{5,4},{6,7},{7,6},{8,9},{9,8},{10,11... | collective-permute-start | bytes 1572872 | tf_op jit(solution)/shard_map/ppermute | solution.py:59
  273.6 20.9 %collective-permute-start.56 = (bf16[128,2048]{1,0:T(8,128)(2,1)S(1)}, bf16[128,2048]{1,0:T(8,128)(2,1)S(1)}, u32[]{:S(2)}, u32[]{:S(2)}) collective-permute-start(bf16[128,2048]{1,0:T(8,128)(2,1)S(1)} %get-tuple-element.19), channel_id=1, source_target_pairs={{0,2},{1,3},{4,0},{5,1},{8,4},{9,5},{12,8},{13,9},{14,12},{15,13},... | collective-permute-start | bytes 1572872 | tf_op jit(solution)/shard_map/ppermute | solution.py:56
  283.3 14.9 %collective-permute-start.63 = (bf16[128,2048]{1,0:T(8,128)(2,1)S(1)}, bf16[128,2048]{1,0:T(8,128)(2,1)S(1)}, u32[]{:S(2)}, u32[]{:S(2)}) collective-permute-start(bf16[128,2048]{1,0:T(8,128)(2,1)S(1)} %get-tuple-element.20), channel_id=1, source_target_pairs={{0,4},{1,5},{4,8},{5,9},{8,12},{9,13},{12,14},{13,15},{14,10},{15,... | collective-permute-start | bytes 1572872 | tf_op jit(solution)/shard_map/ppermute | solution.py:53
  285.5 17.0 %collective-permute-start.24 = (bf16[128,2048]{1,0:T(8,128)(2,1)S(1)}, bf16[128,2048]{1,0:T(8,128)(2,1)S(1)}, u32[]{:S(2)}, u32[]{:S(2)}) collective-permute-start(bf16[128,2048]{1,0:T(8,128)(2,1)S(1)} %get-tuple-element.25), channel_id=1, source_target_pairs={{0,2},{1,3},{4,0},{5,1},{8,4},{9,5},{12,8},{13,9},{14,12},{15,13},... | collective-permute-start | bytes 1572872 | tf_op jit(solution)/shard_map/ppermute | solution.py:56
  285.9 18.0 %collective-permute-start.31 = (bf16[128,2048]{1,0:T(8,128)(2,1)S(1)}, bf16[128,2048]{1,0:T(8,128)(2,1)S(1)}, u32[]{:S(2)}, u32[]{:S(2)}) collective-permute-start(bf16[128,2048]{1,0:T(8,128)(2,1)S(1)} %get-tuple-element.26), channel_id=1, source_target_pairs={{0,4},{1,5},{4,8},{5,9},{8,12},{9,13},{12,14},{13,15},{14,10},{15,... | collective-permute-start | bytes 1572872 | tf_op jit(solution)/shard_map/ppermute | solution.py:53
  (28 other events, 225.8 us)

commit v3 on v2

v3 whole, which is shorter than its diff:
```python
import jax
import jax.numpy as jnp
import numpy as np
from jax import lax
from jax.sharding import PartitionSpec as P

F32 = jnp.float32
BF16 = jnp.bfloat16


def ring_order(chips):
    if chips == 8:
        return [0, 2, 4, 6, 7, 5, 3, 1]
    return list(range(chips))


def plan(nodes):
    chips = nodes // 2
    order = ring_order(chips)
    at = {chip: i for i, chip in enumerate(order)}

    def moves(step):
        return [
            (order[i] * 2 + c, order[(i + step) % chips] * 2 + c)
            for i in range(chips)
            for c in range(2)
        ]

    swap = [(i, i ^ 1) for i in range(nodes)]
    half = chips // 2
    groups = [[0]] + [[d, chips - d] for d in range(1, half)] + [[half]]
    slots = [(d, k) for group in groups for k in range(2) for d in group]
    table = np.zeros((nodes, nodes), np.int32)
    for me in range(nodes):
        for j, (d, k) in enumerate(slots):
            table[me, j] = order[(at[me // 2] - d) % chips] * 2 + ((me % 2) ^ k)
    inverse = np.argsort(table, axis=1).astype(np.int32)
    return half, groups, moves(1), moves(-1), swap, table, inverse


def shards(tokens, grad_out, routes, combine_weights, w_gate, w_up, w_down):
    nodes = lax.axis_size("expert")
    per_node = w_gate.shape[0]
    tok_rows, top_count = routes.shape
    width = tokens.shape[1]
    experts = per_node * nodes
    cap = 5 * tok_rows * top_count // (4 * experts)
    mid = tok_rows // 2
    half, groups, right, left, swap, table, inverse = plan(nodes)
    me = lax.axis_index("expert")

    def go_right(rows):
        return lax.ppermute(rows, "expert", right)

    def go_left(rows):
        return lax.ppermute(rows, "expert", left)

    def across(rows):
        return lax.ppermute(rows, "expert", swap)

    def gather_ring(own):
        rings = [[own]]
        from_left, from_right = own, own
        for _ in range(1, half):
            from_left, from_right = go_right(from_left), go_left(from_right)
            rings.append([from_left, from_right])
        last = jnp.concatenate([go_right(from_left[:mid]), go_left(from_right[mid:])], axis=0)
        rings.append([last])
        return rings, (from_left, from_right)

    matches = routes[:, :, None] == jnp.arange(experts, dtype=jnp.int32)[None, None, :]
    dense = jnp.sum(jnp.where(matches, combine_weights[:, :, None], 0.0), axis=1)
    dense = dense.T.reshape(nodes, per_node, tok_rows)
    here = lax.all_gather(dense, "expert")
    here = lax.dynamic_index_in_dim(here, me, axis=1, keepdims=False)
    here = here[jnp.asarray(table)[me]]
    named = here > 0.0
    place = jnp.cumsum(named.astype(jnp.int32), axis=2) - 1
    pick = named[:, :, None, :] & (
        place[:, :, None, :] == jnp.arange(cap, dtype=jnp.int32)[None, None, :, None]
    )
    scale = jnp.sum(jnp.where(pick, here[:, :, None, :], 0.0), axis=3)
    scale = scale.transpose(1, 0, 2)
    hot = pick.astype(BF16).reshape(nodes, per_node * cap, tok_rows)

    starts = [int(v) for v in np.cumsum([0] + [2 * len(group) for group in groups])]
    cut = half - 1
    chunks = [(cut, half + 1), (0, cut)]

    def compact(rings, chunk):
        parts = []
        for number in range(*chunk):
            ring = rings[number]
            rows = jnp.stack(ring + [across(own) for own in ring])
            span = slice(starts[number], starts[number + 1])
            got = jnp.einsum("nct,ntd->ncd", hot[span], rows, preferred_element_type=F32)
            got = got.astype(BF16).reshape(-1, per_node, cap, width)
            parts.append(got.transpose(1, 0, 2, 3).reshape(per_node, -1, width))
        return jnp.concatenate(parts, axis=1)

    def chunk_scale(chunk):
        part = scale[:, starts[chunk[0]]:starts[chunk[1]]]
        return part.reshape(per_node, -1, 1)

    def forward(x, weight):
        gate = jnp.einsum("erd,edf->erf", x, w_gate, preferred_element_type=F32)
        up = jnp.einsum("erd,edf->erf", x, w_up, preferred_element_type=F32)
        hidden = (gate * jax.nn.sigmoid(gate) * up * weight).astype(BF16)
        out = jnp.einsum("erf,efd->erd", hidden, w_down, preferred_element_type=F32)
        return out.astype(BF16), gate, up

    def backward_hidden(pull, gate, up, weight):
        squash = jax.nn.sigmoid(gate)
        act = gate * squash
        dots = jnp.sum(pull * act * up, axis=2).reshape(per_node, -1, cap)
        pull = pull * weight
        gate_grad = (pull * up * squash * (1.0 + gate * (1.0 - squash))).astype(BF16)
        return dots, gate_grad, (pull * act).astype(BF16)

    def backward_rows(gate_grad, up_grad):
        rows = jnp.einsum("erf,edf->erd", gate_grad, w_gate, preferred_element_type=F32)
        rows = rows + jnp.einsum("erf,edf->erd", up_grad, w_up, preferred_element_type=F32)
        return rows.astype(BF16)

    def one(rows, slot, base):
        part = rows[:, (slot - base) * cap:(slot - base + 1) * cap].reshape(-1, width)
        return jnp.einsum("ct,cd->td", hot[slot], part, preferred_element_type=F32)

    def swapped(rows, base, number):
        count = len(groups[number])
        return [
            across(one(rows, starts[number] + count + i, base).astype(BF16)) for i in range(count)
        ]

    def pieces(rows, chunk):
        base = starts[chunk[0]]
        got = {}
        for number in reversed(range(*chunk)):
            got[number] = (rows, base, swapped(rows, base, number))
        return got

    def own_sum(piece, number, i):
        rows, base, other = piece[number]
        return one(rows, starts[number] + i, base) + other[i].astype(F32)

    def far_step(piece):
        far = own_sum(piece, half, 0).astype(BF16)
        blank = jnp.zeros((tok_rows - mid, width), BF16)
        to_left = jnp.concatenate([go_left(far[:mid]), blank], axis=0)
        to_right = jnp.concatenate([blank, go_right(far[mid:])], axis=0)
        return to_left, to_right

    def ring_sum(piece, number, moving):
        to_left = (own_sum(piece, number, 0) + moving[0].astype(F32)).astype(BF16)
        to_right = (own_sum(piece, number, 1) + moving[1].astype(F32)).astype(BF16)
        return to_left, to_right

    def ring_send(moving):
        return go_left(moving[0]), go_right(moving[1])

    def last_sum(piece, moving):
        total = own_sum(piece, 0, 0) + moving[0].astype(F32) + moving[1].astype(F32)
        return total.astype(BF16)

    tie = lax.optimization_barrier
    far_span, near_span = chunks
    scales = [chunk_scale(chunk) for chunk in chunks]

    rings, ends = gather_ring(tokens)
    near_x = compact(rings, near_span)
    far_x = compact(rings, far_span)
    grad_out, _ = tie((grad_out, ends))
    rings, ends = gather_ring(grad_out)
    near_out, near_gate, near_up = forward(near_x, scales[1])
    far_out, far_gate, far_up = forward(far_x, scales[0])
    far_out, near_out, _ = tie((far_out, near_out, ends))

    piece = pieces(far_out, far_span)
    piece.update(pieces(near_out, near_span))
    moving = far_step(piece)
    far_g = compact(rings, far_span)
    near_g = compact(rings, near_span)

    stages = list(range(half - 1, 0, -1))
    moving = ring_sum(piece, stages[0], moving)
    far_g, near_g, moving = tie((far_g, near_g, moving))
    moving = ring_send(moving)

    pull = jnp.einsum("erd,efd->erf", far_g, w_down, preferred_element_type=F32)
    dots_far, gate_grad, up_grad = backward_hidden(tie(pull), far_gate, far_up, scales[0])
    if len(stages) > 1:
        moving = ring_sum(piece, stages[1], moving)
        gate_grad, up_grad, near_g, moving = tie((gate_grad, up_grad, near_g, moving))
        moving = ring_send(moving)
    far_rows = backward_rows(gate_grad, up_grad)
    pull = tie(jnp.einsum("erd,efd->erf", near_g, w_down, preferred_element_type=F32))
    for number in stages[2:]:
        moving = ring_sum(piece, number, moving)
        far_rows, pull, moving = tie((far_rows, pull, moving))
        moving = ring_send(moving)
    back_piece = pieces(far_rows, far_span)
    dots_near, gate_grad, up_grad = backward_hidden(pull, near_gate, near_up, scales[1])
    back = far_step(back_piece)
    near_rows = backward_rows(gate_grad, up_grad)
    combined = last_sum(piece, moving)
    back_piece.update(pieces(near_rows, near_span))
    for number in stages:
        back = ring_send(ring_sum(back_piece, number, back))
    grad_tokens = last_sum(back_piece, back)

    dots = jnp.concatenate([dots_near, dots_far], axis=1).transpose(1, 0, 2)
    dots = jnp.sum(jnp.where(pick, dots[:, :, :, None], 0.0), axis=2)
    dots = dots[jnp.asarray(inverse)[me]]
    sent = lax.all_gather(dots, "expert")
    sent = lax.dynamic_index_in_dim(sent, me, axis=1, keepdims=False)
    sent = sent.reshape(experts, tok_rows).T
    grad_weights = jnp.sum(jnp.where(matches, sent[:, None, :], 0.0), axis=2)
    return (combined, grad_tokens, grad_weights)


def solution(mesh):
    rows = P(("groups", "expert"), None)
    held = P("expert", None, None)
    return jax.shard_map(
        shards,
        mesh=mesh,
        in_specs=(rows, rows, rows, rows, held, held, held),
        out_specs=(rows, rows, rows),
        check_vma=False,
    )
```

time: 310 us -> 324 us (1.045)
  blocking collectives: 0 us -> 47.1 us
  waiting for transfers between devices: 134 us -> 101 us
  local copies, waits for them, and re-layouts: 22.9 us -> 7.28 us
  other arithmetic: 12.9 us -> 26.5 us
  matrix products: 82.4 us -> 86.2 us
    all_gather x0 -> x2, blocking collectives: none -> 47.1 us  [the longest x1 27.5 us: shards(): here = lax.all_gather(dense, 'expert')]
    ppermute x16, waiting for transfers between devices: 76.7 us -> 34.8 us  [go_left(): return lax.ppermute(rows, 'expert', left)]
    ppermute x16, waiting for transfers between devices: 42.6 us -> 63.9 us  [go_right(): return lax.ppermute(rows, 'expert', right)]
    ppermute x16, starting transfers between devices: 20.2 us -> 33.8 us  [go_left(): return lax.ppermute(rows, 'expert', left)]
    all_to_all x2 -> x0, waiting for transfers between devices: 12.6 us -> none  [the longest x1 8.25 us: shards(): lax.all_to_all(dense, 'expert', split_axis=0, concat_axis=0, tiled=True)]
    convert_element_type x10 -> x0, local copies, waits for them, and re-layouts: 10.2 us -> none  [partials(): got[2 * i + 1].astype(BF16)]
    all_to_all x2 -> x0, starting transfers between devices: 9.92 us -> none  [the longest x1 6.43 us: shards(): lax.all_to_all(dense, 'expert', split_axis=0, concat_axis=0, tiled=True)]
    ppermute x16, starting transfers between devices: 15.2 us -> 8.98 us  [go_right(): return lax.ppermute(rows, 'expert', right)]
  transfers between devices with their start and end apart: 66 -> 64, of which waited for: 24 -> 22; matrix products, arithmetic and copies ran while one was open for 20% -> 37% of each run, Pallas kernels for 0% -> 0%
where the time goes in v3:
time: 324 us; the launch traced here: 319 us
  waiting for transfers between devices  101 us (31%)
  matrix products  86.2 us (27%)
  starting transfers between devices  48.3 us (15%)
  blocking collectives  47.1 us (15%)
  other arithmetic  26.5 us (8%)
  local copies, waits for them, and re-layouts  7.28 us (2%)
    ppermute x16, waiting for transfers between devices, go_right(): return lax.ppermute(rows, 'expert', right)  63.9 us
    ppermute x16, waiting for transfers between devices, go_left(): return lax.ppermute(rows, 'expert', left)  34.8 us
    ppermute x16, starting transfers between devices, go_left(): return lax.ppermute(rows, 'expert', left)  33.8 us
    dot_general x32, matrix products, one(): return jnp.einsum('ct,cd->td', hot[slot], part, preferred_element_type=F32)  29.6 us
    all_gather x1, blocking collectives, shards(): here = lax.all_gather(dense, 'expert')  27.5 us
    all_gather x1, blocking collectives, shards(): sent = lax.all_gather(dots, 'expert')  19.6 us
    dot_general x2, matrix products, backward_rows(): jnp.einsum('erf,edf->erd', gate_grad, w_gate, preferred_element_type=F32)  13.3 us
    dot_general x2, matrix products, backward_rows(): jnp.einsum('erf,edf->erd', up_grad, w_up, preferred_element_type=F32)  10.6 us
  transfers between devices with their start and end apart: 64, of which 22 were waited for; matrix products, arithmetic and copies ran while one was open for 37% of the time, Pallas kernels for 0%

profile of v3, /device:TPU:0, one launch (start us, length us, event | category | flops | bytes accessed | tf_op | source)
XLA Modules:
  0.0 318.7 jit_solution(5902442332811483695)
XLA Ops:
  0.6 3.1 collective-permute-start
  4.5 27.5 %all_gather.9 = f32[16,16,2,128]{3,1,2,0:T(8,128)S(1)} all-gather(f32[1,16,2,128]{3,1,2,0:T(8,128)S(1)} %copy.101), channel_id=1, replica_groups=mesh['groups'=2,'expert'=16] {'expert'}, dimensions={0}, use_global_device_ids=true | all-gather | bytes 278528 | tf_op jit(solution)/shard_map/all_gather | solution.py:74
  35.2 2.0 collective-permute-start.4
  38.7 10.6 %collective-permute-done.1 = bf16[128,2048]{1,0:T(8,128)(2,1)S(1)} collective-permute-done((bf16[128,2048]{1,0:T(8,128)(2,1)S(1)}, bf16[128,2048]{1,0:T(8,128)(2,1)S(1)}, u32[]{:S(2)}, u32[]{:S(2)}) %collective-permute-start.1) | collective-permute-done | bytes 524320 | tf_op jit(solution)/shard_map/ppermute | solution.py:53
  49.9 1.4 convolution_convert_fusion.10
  51.7 1.7 convolution_convert_fusion.6
  53.6 1.8 collective-permute-start.5
  56.0 9.2 %collective-permute-done.2 = bf16[128,2048]{1,0:T(8,128)(2,1)S(1)} collective-permute-done((bf16[128,2048]{1,0:T(8,128)(2,1)S(1)}, bf16[128,2048]{1,0:T(8,128)(2,1)S(1)}, u32[]{:S(2)}, u32[]{:S(2)}) %collective-permute-start.2) | collective-permute-done | bytes 524320 | tf_op jit(solution)/shard_map/ppermute | solution.py:53
  65.6 2.7 fusion.45
  68.4 2.7 fusion.44
  71.2 1.8 collective-permute-start.9
  73.8 6.3 %convolution_convert_fusion = bf16[2,400,2048]{2,1,0:T(8,128)(2,1)S(1)} fusion(bf16[2,768,2048]{2,1,0:T(8,128)(2,1)} %param.15, f32[2,400,768]{2,1,0:T(8,128)S(1)} %fusion.44, f32[2,400]{1,0:T(2,128)S(1)} %mul.95, f32[2,400,768]{2,1,0:T(8,128)S(1)} %fusion.45), kind=kOutput, calls=%fused_computation.4 | convolution fusion | flops 2522521600 | bytes 14486656 | tf_op jit(solution)/shard_map/erf,efd->erd/dot_general | solution.py:109
  80.2 1.8 collective-permute-start.19
  84.4 1.6 collective-permute-done.16
  86.3 7.8 %collective-permute-done.19 = bf16[128,2048]{1,0:T(8,128)(2,1)S(1)} collective-permute-done((bf16[128,2048]{1,0:T(8,128)(2,1)S(1)}, bf16[128,2048]{1,0:T(8,128)(2,1)S(1)}, u32[]{:S(2)}, u32[]{:S(2)}) %collective-permute-start.19) | collective-permute-done | bytes 524320 | tf_op jit(solution)/shard_map/ppermute | solution.py:56
  94.1 2.0 collective-permute-start.20
  96.6 1.7 fusion.47
  98.3 1.7 fusion.46
  100.3 7.1 %collective-permute-done.20 = bf16[128,2048]{1,0:T(8,128)(2,1)S(1)} collective-permute-done((bf16[128,2048]{1,0:T(8,128)(2,1)S(1)}, bf16[128,2048]{1,0:T(8,128)(2,1)S(1)}, u32[]{:S(2)}, u32[]{:S(2)}) %collective-permute-start.20) | collective-permute-done | bytes 524320 | tf_op jit(solution)/shard_map/ppermute | solution.py:56
  107.4 1.7 collective-permute-start.21
  109.2 2.0 convolution_convert_fusion.1
  112.4 2.0 collective-permute-done.18
  114.3 5.2 %collective-permute-done.21 = bf16[128,2048]{1,0:T(8,128)(2,1)S(1)} collective-permute-done((bf16[128,2048]{1,0:T(8,128)(2,1)S(1)}, bf16[128,2048]{1,0:T(8,128)(2,1)S(1)}, u32[]{:S(2)}, u32[]{:S(2)}) %collective-permute-start.21) | collective-permute-done | bytes 524320 | tf_op jit(solution)/shard_map/ppermute | solution.py:56
  122.8 1.9 collective-permute-start.26
  130.1 1.4 fusion.105
  131.8 1.8 pad_maximum_fusion.1
  139.5 1.9 collective-permute-start.35
  142.0 5.0 %collective-permute-done.37 = bf16[64,2048]{1,0:T(8,128)(2,1)S(1)} collective-permute-done((bf16[64,2048]{1,0:T(8,128)(2,1)S(1)}, bf16[64,2048]{1,0:T(8,128)(2,1)S(1)}, u32[]{:S(2)}, u32[]{:S(2)}) %collective-permute-start.37) | collective-permute-done | bytes 262176 | tf_op jit(solution)/shard_map/ppermute | solution.py:53
  149.7 1.6 collective-permute-start.39
  151.3 1.8 fusion.100
  153.1 2.1 multiply_reduce_fusion.1
  155.9 8.0 %collective-permute-done.41 = bf16[128,2048]{1,0:T(8,128)(2,1)} collective-permute-done((bf16[128,2048]{1,0:T(8,128)(2,1)}, bf16[128,2048]{1,0:T(8,128)(2,1)}, u32[]{:S(2)}, u32[]{:S(2)}) %collective-permute-start.41) | collective-permute-done | bytes 524320 | tf_op jit(solution)/shard_map/ppermute | solution.py:53
  164.0 2.2 add_convert_fusion.13
  166.1 2.2 add_convert_fusion.14
  168.6 10.2 %collective-permute-start.43 = (bf16[128,2048]{1,0:T(8,128)(2,1)}, bf16[128,2048]{1,0:T(8,128)(2,1)S(1)}, u32[]{:S(2)}, u32[]{:S(2)}) collective-permute-start(bf16[128,2048]{1,0:T(8,128)(2,1)} %add_convert_fusion.14), channel_id=1, source_target_pairs={{0,2},{1,3},{4,0},{5,1},{8,4},{9,5},{12,8},{13,9},{14,12},{15,13},... | collective-permute-start | bytes 1572872 | tf_op jit(solution)/shard_map/ppermute | solution.py:56
  178.8 4.8 %fusion.103 = f32[2,240,2048]{2,1,0:T(8,128)S(1)} fusion(bf16[2,240,768]{2,1,0:T(8,128)(2,1)S(1)} %copy-done.5, bf16[2,2048,768]{2,1,0:T(8,128)(2,1)} %param.13), kind=kOutput, calls=%fused_computation.183 | convolution fusion | flops 1509949440 | bytes 10960896 | tf_op jit(solution)/shard_map/erf,edf->erd/dot_general | solution.py:121
  183.7 7.2 %fusion.104 = f32[2,400,768]{2,1,0:T(8,128)} fusion(bf16[2,400,2048]{2,1,0:T(8,128)(2,1)S(1)} %copy-done.3, bf16[2,768,2048]{2,1,0:T(8,128)(2,1)} %param.15), kind=kOutput, calls=%fused_computation.184 | convolution fusion | flops 2516582400 | bytes 12025856 | tf_op jit(solution)/shard_map/erd,efd->erf/dot_general | solution.py:196
  190.9 1.8 add_convert_fusion.1
  192.8 2.3 add_convert_fusion.11
  195.2 2.0 add_convert_fusion.12
  197.2 3.2 %multiply_reduce_fusion = f32[2,400]{1,0:T(2,128)S(1)} fusion(f32[2,400,768]{2,1,0:T(8,128)} %copy-done.9, f32[2,400,768]{2,1,0:T(8,128)} %fusion.104, f32[2,400,768]{2,1,0:T(8,128)S(1)} %copy-done.7), kind=kLoop, calls=%fused_computation.14 | loop fusion | flops 4300000 | bytes 7376000 | tf_op jit(solution)/shard_map/reduce_sum | solution.py:115
  200.5 8.5 %fusion.48 = f32[2,400,2048]{2,1,0:T(8,128)} fusion(bf16[2,2048,768]{2,1,0:T(8,128)(2,1)S(1)} %bitcast.249, f32[2,400,768]{2,1,0:T(8,128)S(1)} %copy-done.7, f32[2,400,768]{2,1,0:T(8,128)} %copy-done.9, f32[2,400,768]{2,1,0:T(8,128)} %fusion.104, f32[2,400]{1,0:T(2,128)S(1)} %copy-done.59), kind=kOutput, calls=%fused_computation.94 | convolution fusion | flops 2523340800 | bytes 20221056 | tf_op jit(solution)/shard_map/erf,edf->erd/dot_general | solution.py:121
  213.0 8.8 %add_convert_fusion = bf16[2,400,2048]{2,1,0:T(8,128)(2,1)S(1)} fusion(f32[2,400,2048]{2,1,0:T(8,128)} %fusion.48, bf16[2,2048,768]{2,1,0:T(8,128)(2,1)} %param.14, f32[2,400,768]{2,1,0:T(8,128)} %fusion.104, f32[2,400]{1,0:T(2,128)S(1)} %copy-done.59, f32[2,400,768]{2,1,0:T(8,128)S(1)} %copy-done.8), kind=kOutput, calls=%fused_computation.2 | convolution fusion | flops 2524160000 | bytes 21040256 | tf_op jit(solution)/shard_map/erf,edf->erd/dot_general | solution.py:122
  231.1 1.4 gather_fusion.1
  232.6 1.4 fusion.110
  235.4 1.4 add_convert_fusion.9
  236.9 1.8 collective-permute-start.53
  239.0 19.6 %all-gather = f32[256,2,128]{2,1,0:T(2,128)S(1)} all-gather(f32[16,2,128]{2,1,0:T(2,128)S(1)} %gather_fusion.1), channel_id=2, replica_groups=mesh['groups'=2,'expert'=16] {'expert'}, dimensions={0}, use_global_device_ids=true | all-gather | bytes 278528 | tf_op jit(solution)/shard_map/all_gather | solution.py:214
  258.8 1.4 add_convert_fusion.8
  260.2 2.0 collective-permute-start.54
  262.6 4.6 %collective-permute-done.60 = bf16[64,2048]{1,0:T(8,128)(2,1)S(1)} collective-permute-done((bf16[64,2048]{1,0:T(8,128)(2,1)S(1)}, bf16[64,2048]{1,0:T(8,128)(2,1)S(1)}, u32[]{:S(2)}, u32[]{:S(2)}) %collective-permute-start.60) | collective-permute-done | bytes 262176 | tf_op jit(solution)/shard_map/ppermute | solution.py:53
  267.3 1.4 add_convert_fusion.5
  269.2 5.2 %collective-permute-done.54 = bf16[128,2048]{1,0:T(8,128)(2,1)S(1)} collective-permute-done((bf16[128,2048]{1,0:T(8,128)(2,1)S(1)}, bf16[128,2048]{1,0:T(8,128)(2,1)S(1)}, u32[]{:S(2)}, u32[]{:S(2)}) %collective-permute-start.54) | collective-permute-done | bytes 524320 | tf_op jit(solution)/shard_map/ppermute | solution.py:56
  275.6 1.8 collective-permute-start.55
  277.4 4.7 %collective-permute-done.61 = bf16[128,2048]{1,0:T(8,128)(2,1)S(1)} collective-permute-done((bf16[128,2048]{1,0:T(8,128)(2,1)S(1)}, bf16[128,2048]{1,0:T(8,128)(2,1)S(1)}, u32[]{:S(2)}, u32[]{:S(2)}) %collective-permute-start.61) | collective-permute-done | bytes 524320 | tf_op jit(solution)/shard_map/ppermute | solution.py:53
  283.5 1.5 collective-permute-start.46
  285.0 5.4 %collective-permute-done.55 = bf16[128,2048]{1,0:T(8,128)(2,1)S(1)} collective-permute-done((bf16[128,2048]{1,0:T(8,128)(2,1)S(1)}, bf16[128,2048]{1,0:T(8,128)(2,1)S(1)}, u32[]{:S(2)}, u32[]{:S(2)}) %collective-permute-start.55) | collective-permute-done | bytes 524320 | tf_op jit(solution)/shard_map/ppermute | solution.py:56
  290.7 6.5 %collective-permute-done.62 = bf16[128,2048]{1,0:T(8,128)(2,1)S(1)} collective-permute-done((bf16[128,2048]{1,0:T(8,128)(2,1)S(1)}, bf16[128,2048]{1,0:T(8,128)(2,1)S(1)}, u32[]{:S(2)}, u32[]{:S(2)}) %collective-permute-start.62) | collective-permute-done | bytes 524320 | tf_op jit(solution)/shard_map/ppermute | solution.py:53
  297.5 2.1 collective-permute-start.63
  299.5 2.1 collective-permute-done.46
  301.6 6.8 %collective-permute-done.47 = bf16[128,2048]{1,0:T(8,128)(2,1)S(1)} collective-permute-done((bf16[128,2048]{1,0:T(8,128)(2,1)S(1)}, bf16[128,2048]{1,0:T(8,128)(2,1)S(1)}, u32[]{:S(2)}, u32[]{:S(2)}) %collective-permute-start.47) | collective-permute-done | bytes 524320 | tf_op jit(solution)/shard_map/ppermute | solution.py:53
  308.5 2.1 add_convert_fusion.10
  310.6 1.9 collective-permute-done.56
  312.5 4.8 %collective-permute-done.63 = bf16[128,2048]{1,0:T(8,128)(2,1)S(1)} collective-permute-done((bf16[128,2048]{1,0:T(8,128)(2,1)S(1)}, bf16[128,2048]{1,0:T(8,128)(2,1)S(1)}, u32[]{:S(2)}, u32[]{:S(2)}) %collective-permute-start.63) | collective-permute-done | bytes 524320 | tf_op jit(solution)/shard_map/ppermute | solution.py:53
  (336 shorter events, 52.1 us)
Async XLA Ops:
  0.6 34.5 %collective-permute-start = (bf16[128,2048]{1,0:T(8,128)(2,1)}, bf16[128,2048]{1,0:T(8,128)(2,1)S(1)}, u32[]{:S(2)}, u32[]{:S(2)}) collective-permute-start(bf16[128,2048]{1,0:T(8,128)(2,1)} %param.9), channel_id=1, source_target_pairs={{0,4},{1,5},{4,8},{5,9},{8,12},{9,13},{12,14},{13,15},{14,10},{15,... | collective-permute-start | bytes 1572872 | tf_op jit(solution)/shard_map/ppermute | solution.py:53
  3.7 31.5 %collective-permute-start.3 = (bf16[128,2048]{1,0:T(8,128)(2,1)}, bf16[128,2048]{1,0:T(8,128)(2,1)S(1)}, u32[]{:S(2)}, u32[]{:S(2)}) collective-permute-start(bf16[128,2048]{1,0:T(8,128)(2,1)} %param.9), channel_id=1, source_target_pairs={{0,2},{1,3},{4,0},{5,1},{8,4},{9,5},{12,8},{13,9},{14,12},{15,13},... | collective-permute-start | bytes 1572872 | tf_op jit(solution)/shard_map/ppermute | solution.py:56
  3.7 46.2 %collective-permute-start.11 = (bf16[128,2048]{1,0:T(8,128)(2,1)}, bf16[128,2048]{1,0:T(8,128)(2,1)S(1)}, u32[]{:S(2)}, u32[]{:S(2)}) collective-permute-start(bf16[128,2048]{1,0:T(8,128)(2,1)} %param.9), channel_id=1, source_target_pairs={{0,1},{1,0},{2,3},{3,2},{4,5},{5,4},{6,7},{7,6},{8,9},{9,8},{10,11... | collective-permute-start | bytes 1572872 | tf_op jit(solution)/shard_map/ppermute | solution.py:59
  35.1 14.2 %collective-permute-start.1 = (bf16[128,2048]{1,0:T(8,128)(2,1)S(1)}, bf16[128,2048]{1,0:T(8,128)(2,1)S(1)}, u32[]{:S(2)}, u32[]{:S(2)}) collective-permute-start(bf16[128,2048]{1,0:T(8,128)(2,1)S(1)} %collective-permute-done), channel_id=1, source_target_pairs={{0,4},{1,5},{4,8},{5,9},{8,12},{9,13},{12,14},{13,15},{14,10},{15,... | collective-permute-start | bytes 1572872 | tf_op jit(solution)/shard_map/ppermute | solution.py:53
  35.2 14.2 %collective-permute-start.4 = (bf16[128,2048]{1,0:T(8,128)(2,1)S(1)}, bf16[128,2048]{1,0:T(8,128)(2,1)S(1)}, u32[]{:S(2)}, u32[]{:S(2)}) collective-permute-start(bf16[128,2048]{1,0:T(8,128)(2,1)S(1)} %collective-permute-done.3), channel_id=1, source_target_pairs={{0,2},{1,3},{4,0},{5,1},{8,4},{9,5},{12,8},{13,9},{14,12},{15,13},... | collective-permute-start | bytes 1572872 | tf_op jit(solution)/shard_map/ppermute | solution.py:56
  37.2 14.4 %collective-permute-start.12 = (bf16[128,2048]{1,0:T(8,128)(2,1)S(1)}, bf16[128,2048]{1,0:T(8,128)(2,1)}, u32[]{:S(2)}, u32[]{:S(2)}) collective-permute-start(bf16[128,2048]{1,0:T(8,128)(2,1)S(1)} %collective-permute-done), channel_id=1, source_target_pairs={{0,1},{1,0},{2,3},{3,2},{4,5},{5,4},{6,7},{7,6},{8,9},{9,8},{10,11... | collective-permute-start | bytes 1572872 | tf_op jit(solution)/shard_map/ppermute | solution.py:59
  37.2 14.4 %collective-permute-start.13 = (bf16[128,2048]{1,0:T(8,128)(2,1)S(1)}, bf16[128,2048]{1,0:T(8,128)(2,1)}, u32[]{:S(2)}, u32[]{:S(2)}) collective-permute-start(bf16[128,2048]{1,0:T(8,128)(2,1)S(1)} %collective-permute-done.3), channel_id=1, source_target_pairs={{0,1},{1,0},{2,3},{3,2},{4,5},{5,4},{6,7},{7,6},{8,9},{9,8},{10,11... | collective-permute-start | bytes 1572872 | tf_op jit(solution)/shard_map/ppermute | solution.py:59
  49.4 6.0 %collective-permute-start.14 = (bf16[128,2048]{1,0:T(8,128)(2,1)S(1)}, bf16[128,2048]{1,0:T(8,128)(2,1)S(1)}, u32[]{:S(2)}, u32[]{:S(2)}) collective-permute-start(bf16[128,2048]{1,0:T(8,128)(2,1)S(1)} %collective-permute-done.1), channel_id=1, source_target_pairs={{0,1},{1,0},{2,3},{3,2},{4,5},{5,4},{6,7},{7,6},{8,9},{9,8},{10,11... | collective-permute-start | bytes 1572872 | tf_op jit(solution)/shard_map/ppermute | solution.py:59
  49.4 5.9 %collective-permute-start.15 = (bf16[128,2048]{1,0:T(8,128)(2,1)S(1)}, bf16[128,2048]{1,0:T(8,128)(2,1)S(1)}, u32[]{:S(2)}, u32[]{:S(2)}) collective-permute-start(bf16[128,2048]{1,0:T(8,128)(2,1)S(1)} %collective-permute-done.4), channel_id=1, source_target_pairs={{0,1},{1,0},{2,3},{3,2},{4,5},{5,4},{6,7},{7,6},{8,9},{9,8},{10,11... | collective-permute-start | bytes 1572872 | tf_op jit(solution)/shard_map/ppermute | solution.py:59
  51.3 14.0 %collective-permute-start.2 = (bf16[128,2048]{1,0:T(8,128)(2,1)S(1)}, bf16[128,2048]{1,0:T(8,128)(2,1)S(1)}, u32[]{:S(2)}, u32[]{:S(2)}) collective-permute-start(bf16[128,2048]{1,0:T(8,128)(2,1)S(1)} %collective-permute-done.1), channel_id=1, source_target_pairs={{0,4},{1,5},{4,8},{5,9},{8,12},{9,13},{12,14},{13,15},{14,10},{15,... | collective-permute-start | bytes 1572872 | tf_op jit(solution)/shard_map/ppermute | solution.py:53
  53.6 17.6 %collective-permute-start.5 = (bf16[128,2048]{1,0:T(8,128)(2,1)S(1)}, bf16[128,2048]{1,0:T(8,128)(2,1)S(1)}, u32[]{:S(2)}, u32[]{:S(2)}) collective-permute-start(bf16[128,2048]{1,0:T(8,128)(2,1)S(1)} %collective-permute-done.4), channel_id=1, source_target_pairs={{0,2},{1,3},{4,0},{5,1},{8,4},{9,5},{12,8},{13,9},{14,12},{15,13},... | collective-permute-start | bytes 1572872 | tf_op jit(solution)/shard_map/ppermute | solution.py:56
  65.3 14.9 %collective-permute-start.8 = (bf16[64,2048]{1,0:T(8,128)(2,1)S(1)}, bf16[64,2048]{1,0:T(8,128)(2,1)S(1)}, u32[]{:S(2)}, u32[]{:S(2)}) collective-permute-start(bf16[64,2048]{1,0:T(8,128)(2,1)S(1)} %slice.316), channel_id=1, source_target_pairs={{0,4},{1,5},{4,8},{5,9},{8,12},{9,13},{12,14},{13,15},{14,10},{15,... | collective-permute-start | bytes 786440 | tf_op jit(solution)/shard_map/ppermute | solution.py:53
  71.2 10.8 %collective-permute-start.9 = (bf16[64,2048]{1,0:T(8,128)(2,1)S(1)}, bf16[64,2048]{1,0:T(8,128)(2,1)S(1)}, u32[]{:S(2)}, u32[]{:S(2)}) collective-permute-start(bf16[64,2048]{1,0:T(8,128)(2,1)S(1)} %slice.317), channel_id=1, source_target_pairs={{0,2},{1,3},{4,0},{5,1},{8,4},{9,5},{12,8},{13,9},{14,12},{15,13},... | collective-permute-start | bytes 786440 | tf_op jit(solution)/shard_map/ppermute | solution.py:56
  73.0 13.0 %collective-permute-start.16 = (bf16[128,2048]{1,0:T(8,128)(2,1)S(1)}, bf16[128,2048]{1,0:T(8,128)(2,1)S(1)}, u32[]{:S(2)}, u32[]{:S(2)}) collective-permute-start(bf16[128,2048]{1,0:T(8,128)(2,1)S(1)} %copy-done.17), channel_id=1, source_target_pairs={{0,4},{1,5},{4,8},{5,9},{8,12},{9,13},{12,14},{13,15},{14,10},{15,... | collective-permute-start | bytes 1572872 | tf_op jit(solution)/shard_map/ppermute | solution.py:53
  73.3 8.8 %collective-permute-start.7 = (bf16[128,2048]{1,0:T(8,128)(2,1)S(1)}, bf16[128,2048]{1,0:T(8,128)(2,1)S(1)}, u32[]{:S(2)}, u32[]{:S(2)}) collective-permute-start(bf16[128,2048]{1,0:T(8,128)(2,1)S(1)} %collective-permute-done.5), channel_id=1, source_target_pairs={{0,1},{1,0},{2,3},{3,2},{4,5},{5,4},{6,7},{7,6},{8,9},{9,8},{10,11... | collective-permute-start | bytes 1572872 | tf_op jit(solution)/shard_map/ppermute | solution.py:59
  73.3 9.4 %collective-permute-start.6 = (bf16[128,2048]{1,0:T(8,128)(2,1)S(1)}, bf16[128,2048]{1,0:T(8,128)(2,1)S(1)}, u32[]{:S(2)}, u32[]{:S(2)}) collective-permute-start(bf16[128,2048]{1,0:T(8,128)(2,1)S(1)} %collective-permute-done.2), channel_id=1, source_target_pairs={{0,1},{1,0},{2,3},{3,2},{4,5},{5,4},{6,7},{7,6},{8,9},{9,8},{10,11... | collective-permute-start | bytes 1572872 | tf_op jit(solution)/shard_map/ppermute | solution.py:59
  80.2 13.9 %collective-permute-start.19 = (bf16[128,2048]{1,0:T(8,128)(2,1)S(1)}, bf16[128,2048]{1,0:T(8,128)(2,1)S(1)}, u32[]{:S(2)}, u32[]{:S(2)}) collective-permute-start(bf16[128,2048]{1,0:T(8,128)(2,1)S(1)} %copy-done.17), channel_id=1, source_target_pairs={{0,2},{1,3},{4,0},{5,1},{8,4},{9,5},{12,8},{13,9},{14,12},{15,13},... | collective-permute-start | bytes 1572872 | tf_op jit(solution)/shard_map/ppermute | solution.py:56
  82.0 2.0 collective-permute-start.28
  82.1 14.0 %collective-permute-start.10 = (bf16[128,2048]{1,0:T(8,128)(2,1)S(1)}, bf16[128,2048]{1,0:T(8,128)(2,1)S(1)}, u32[]{:S(2)}, u32[]{:S(2)}) collective-permute-start(bf16[128,2048]{1,0:T(8,128)(2,1)S(1)} %constant_dynamic-update-slice_fusion), channel_id=1, source_target_pairs={{0,1},{1,0},{2,3},{3,2},{4,5},{5,4},{6,7},{7,6},{8,9},{9,8},{10,11... | collective-permute-start | bytes 1572872 | tf_op jit(solution)/shard_map/ppermute | solution.py:59
  86.0 14.0 %collective-permute-start.17 = (bf16[128,2048]{1,0:T(8,128)(2,1)S(1)}, bf16[128,2048]{1,0:T(8,128)(2,1)S(1)}, u32[]{:S(2)}, u32[]{:S(2)}) collective-permute-start(bf16[128,2048]{1,0:T(8,128)(2,1)S(1)} %collective-permute-done.16), channel_id=1, source_target_pairs={{0,4},{1,5},{4,8},{5,9},{8,12},{9,13},{12,14},{13,15},{14,10},{15,... | collective-permute-start | bytes 1572872 | tf_op jit(solution)/shard_map/ppermute | solution.py:53
  86.3 24.9 %collective-permute-start.29 = (bf16[128,2048]{1,0:T(8,128)(2,1)S(1)}, bf16[128,2048]{1,0:T(8,128)(2,1)S(1)}, u32[]{:S(2)}, u32[]{:S(2)}) collective-permute-start(bf16[128,2048]{1,0:T(8,128)(2,1)S(1)} %collective-permute-done.16), channel_id=1, source_target_pairs={{0,1},{1,0},{2,3},{3,2},{4,5},{5,4},{6,7},{7,6},{8,9},{9,8},{10,11... | collective-permute-start | bytes 1572872 | tf_op jit(solution)/shard_map/ppermute | solution.py:59
  94.1 13.3 %collective-permute-start.20 = (bf16[128,2048]{1,0:T(8,128)(2,1)S(1)}, bf16[128,2048]{1,0:T(8,128)(2,1)S(1)}, u32[]{:S(2)}, u32[]{:S(2)}) collective-permute-start(bf16[128,2048]{1,0:T(8,128)(2,1)S(1)} %collective-permute-done.19), channel_id=1, source_target_pairs={{0,2},{1,3},{4,0},{5,1},{8,4},{9,5},{12,8},{13,9},{14,12},{15,13},... | collective-permute-start | bytes 1572872 | tf_op jit(solution)/shard_map/ppermute | solution.py:56
  96.1 15.0 %collective-permute-start.30 = (bf16[128,2048]{1,0:T(8,128)(2,1)S(1)}, bf16[128,2048]{1,0:T(8,128)(2,1)S(1)}, u32[]{:S(2)}, u32[]{:S(2)}) collective-permute-start(bf16[128,2048]{1,0:T(8,128)(2,1)S(1)} %collective-permute-done.19), channel_id=1, source_target_pairs={{0,1},{1,0},{2,3},{3,2},{4,5},{5,4},{6,7},{7,6},{8,9},{9,8},{10,11... | collective-permute-start | bytes 1572872 | tf_op jit(solution)/shard_map/ppermute | solution.py:59
  100.0 14.4 %collective-permute-start.18 = (bf16[128,2048]{1,0:T(8,128)(2,1)S(1)}, bf16[128,2048]{1,0:T(8,128)(2,1)S(1)}, u32[]{:S(2)}, u32[]{:S(2)}) collective-permute-start(bf16[128,2048]{1,0:T(8,128)(2,1)S(1)} %collective-permute-done.17), channel_id=1, source_target_pairs={{0,4},{1,5},{4,8},{5,9},{8,12},{9,13},{12,14},{13,15},{14,10},{15,... | collective-permute-start | bytes 1572872 | tf_op jit(solution)/shard_map/ppermute | solution.py:53
  107.4 12.1 %collective-permute-start.21 = (bf16[128,2048]{1,0:T(8,128)(2,1)S(1)}, bf16[128,2048]{1,0:T(8,128)(2,1)S(1)}, u32[]{:S(2)}, u32[]{:S(2)}) collective-permute-start(bf16[128,2048]{1,0:T(8,128)(2,1)S(1)} %collective-permute-done.20), channel_id=1, source_target_pairs={{0,2},{1,3},{4,0},{5,1},{8,4},{9,5},{12,8},{13,9},{14,12},{15,13},... | collective-permute-start | bytes 1572872 | tf_op jit(solution)/shard_map/ppermute | solution.py:56
  111.8 10.0 %collective-permute-start.31 = (bf16[128,2048]{1,0:T(8,128)(2,1)S(1)}, bf16[128,2048]{1,0:T(8,128)(2,1)S(1)}, u32[]{:S(2)}, u32[]{:S(2)}) collective-permute-start(bf16[128,2048]{1,0:T(8,128)(2,1)S(1)} %collective-permute-done.17), channel_id=1, source_target_pairs={{0,1},{1,0},{2,3},{3,2},{4,5},{5,4},{6,7},{7,6},{8,9},{9,8},{10,11... | collective-permute-start | bytes 1572872 | tf_op jit(solution)/shard_map/ppermute | solution.py:59
  111.9 9.9 %collective-permute-start.32 = (bf16[128,2048]{1,0:T(8,128)(2,1)S(1)}, bf16[128,2048]{1,0:T(8,128)(2,1)S(1)}, u32[]{:S(2)}, u32[]{:S(2)}) collective-permute-start(bf16[128,2048]{1,0:T(8,128)(2,1)S(1)} %collective-permute-done.20), channel_id=1, source_target_pairs={{0,1},{1,0},{2,3},{3,2},{4,5},{5,4},{6,7},{7,6},{8,9},{9,8},{10,11... | collective-permute-start | bytes 1572872 | tf_op jit(solution)/shard_map/ppermute | solution.py:59
  120.4 16.2 %collective-permute-start.34 = (bf16[128,2048]{1,0:T(8,128)(2,1)S(1)}, bf16[128,2048]{1,0:T(8,128)(2,1)S(1)}, u32[]{:S(2)}, u32[]{:S(2)}) collective-permute-start(bf16[128,2048]{1,0:T(8,128)(2,1)S(1)} %convolution_convert_fusion.25), channel_id=1, source_target_pairs={{0,1},{1,0},{2,3},{3,2},{4,5},{5,4},{6,7},{7,6},{8,9},{9,8},{10,11... | collective-permute-start | bytes 1572872 | tf_op jit(solution)/shard_map/ppermute | solution.py:59
  120.8 21.1 %collective-permute-start.36 = (bf16[128,2048]{1,0:T(8,128)(2,1)S(1)}, bf16[128,2048]{1,0:T(8,128)(2,1)S(1)}, u32[]{:S(2)}, u32[]{:S(2)}) collective-permute-start(bf16[128,2048]{1,0:T(8,128)(2,1)S(1)} %convolution_convert_fusion.24), channel_id=1, source_target_pairs={{0,1},{1,0},{2,3},{3,2},{4,5},{5,4},{6,7},{7,6},{8,9},{9,8},{10,11... | collective-permute-start | bytes 1572872 | tf_op jit(solution)/shard_map/ppermute | solution.py:59
  121.7 26.4 %collective-permute-start.33 = (bf16[128,2048]{1,0:T(8,128)(2,1)S(1)}, bf16[128,2048]{1,0:T(8,128)(2,1)S(1)}, u32[]{:S(2)}, u32[]{:S(2)}) collective-permute-start(bf16[128,2048]{1,0:T(8,128)(2,1)S(1)} %convolution_convert_fusion.26), channel_id=1, source_target_pairs={{0,1},{1,0},{2,3},{3,2},{4,5},{5,4},{6,7},{7,6},{8,9},{9,8},{10,11... | collective-permute-start | bytes 1572872 | tf_op jit(solution)/shard_map/ppermute | solution.py:59
  122.5 13.5 %collective-permute-start.25 = (bf16[64,2048]{1,0:T(8,128)(2,1)S(1)}, bf16[64,2048]{1,0:T(8,128)(2,1)S(1)}, u32[]{:S(2)}, u32[]{:S(2)}) collective-permute-start(bf16[64,2048]{1,0:T(8,128)(2,1)S(1)} %slice.324), channel_id=1, source_target_pairs={{0,4},{1,5},{4,8},{5,9},{8,12},{9,13},{12,14},{13,15},{14,10},{15,... | collective-permute-start | bytes 786440 | tf_op jit(solution)/shard_map/ppermute | solution.py:53
  122.8 13.2 %collective-permute-start.26 = (bf16[64,2048]{1,0:T(8,128)(2,1)S(1)}, bf16[64,2048]{1,0:T(8,128)(2,1)S(1)}, u32[]{:S(2)}, u32[]{:S(2)}) collective-permute-start(bf16[64,2048]{1,0:T(8,128)(2,1)S(1)} %slice.325), channel_id=1, source_target_pairs={{0,2},{1,3},{4,0},{5,1},{8,4},{9,5},{12,8},{13,9},{14,12},{15,13},... | collective-permute-start | bytes 786440 | tf_op jit(solution)/shard_map/ppermute | solution.py:56
  136.0 1.9 collective-permute-start.23
  136.0 2.6 collective-permute-start.24
  136.6 2.9 collective-permute-start.27
  137.9 18.1 %collective-permute-start.40 = (bf16[128,2048]{1,0:T(8,128)(2,1)}, bf16[128,2048]{1,0:T(8,128)(2,1)}, u32[]{:S(2)}, u32[]{:S(2)}) collective-permute-start(bf16[128,2048]{1,0:T(8,128)(2,1)} %convolution_convert_fusion.22), channel_id=1, source_target_pairs={{0,1},{1,0},{2,3},{3,2},{4,5},{5,4},{6,7},{7,6},{8,9},{9,8},{10,11... | collective-permute-start | bytes 1572872 | tf_op jit(solution)/shard_map/ppermute | solution.py:59
  138.6 8.3 %collective-permute-start.37 = (bf16[64,2048]{1,0:T(8,128)(2,1)S(1)}, bf16[64,2048]{1,0:T(8,128)(2,1)S(1)}, u32[]{:S(2)}, u32[]{:S(2)}) collective-permute-start(bf16[64,2048]{1,0:T(8,128)(2,1)S(1)} %get-tuple-element.74), channel_id=1, source_target_pairs={{0,4},{1,5},{4,8},{5,9},{8,12},{9,13},{12,14},{13,15},{14,10},{15,... | collective-permute-start | bytes 786440 | tf_op jit(solution)/shard_map/ppermute | solution.py:53
  139.5 8.7 %collective-permute-start.35 = (bf16[64,2048]{1,0:T(8,128)(2,1)S(1)}, bf16[64,2048]{1,0:T(8,128)(2,1)S(1)}, u32[]{:S(2)}, u32[]{:S(2)}) collective-permute-start(bf16[64,2048]{1,0:T(8,128)(2,1)S(1)} %get-tuple-element.75), channel_id=1, source_target_pairs={{0,2},{1,3},{4,0},{5,1},{8,4},{9,5},{12,8},{13,9},{14,12},{15,13},... | collective-permute-start | bytes 786440 | tf_op jit(solution)/shard_map/ppermute | solution.py:56
  141.9 24.3 %collective-permute-start.38 = (bf16[128,2048]{1,0:T(8,128)(2,1)}, bf16[128,2048]{1,0:T(8,128)(2,1)}, u32[]{:S(2)}, u32[]{:S(2)}) collective-permute-start(bf16[128,2048]{1,0:T(8,128)(2,1)} %convolution_convert_fusion.23), channel_id=1, source_target_pairs={{0,1},{1,0},{2,3},{3,2},{4,5},{5,4},{6,7},{7,6},{8,9},{9,8},{10,11... | collective-permute-start | bytes 1572872 | tf_op jit(solution)/shard_map/ppermute | solution.py:59
  147.0 45.8 %collective-permute-start.44 = (bf16[128,2048]{1,0:T(8,128)(2,1)}, bf16[128,2048]{1,0:T(8,128)(2,1)}, u32[]{:S(2)}, u32[]{:S(2)}) collective-permute-start(bf16[128,2048]{1,0:T(8,128)(2,1)} %convolution_convert_fusion.20), channel_id=1, source_target_pairs={{0,1},{1,0},{2,3},{3,2},{4,5},{5,4},{6,7},{7,6},{8,9},{9,8},{10,11... | collective-permute-start | bytes 1572872 | tf_op jit(solution)/shard_map/ppermute | solution.py:59
  149.3 14.7 %collective-permute-start.41 = (bf16[128,2048]{1,0:T(8,128)(2,1)}, bf16[128,2048]{1,0:T(8,128)(2,1)}, u32[]{:S(2)}, u32[]{:S(2)}) collective-permute-start(bf16[128,2048]{1,0:T(8,128)(2,1)} %add_convert_fusion.15), channel_id=1, source_target_pairs={{0,4},{1,5},{4,8},{5,9},{8,12},{9,13},{12,14},{13,15},{14,10},{15,... | collective-permute-start | bytes 1572872 | tf_op jit(solution)/shard_map/ppermute | solution.py:53
  149.7 16.4 %collective-permute-start.39 = (bf16[128,2048]{1,0:T(8,128)(2,1)}, bf16[128,2048]{1,0:T(8,128)(2,1)}, u32[]{:S(2)}, u32[]{:S(2)}) collective-permute-start(bf16[128,2048]{1,0:T(8,128)(2,1)} %add_convert_fusion.16), channel_id=1, source_target_pairs={{0,2},{1,3},{4,0},{5,1},{8,4},{9,5},{12,8},{13,9},{14,12},{15,13},... | collective-permute-start | bytes 1572872 | tf_op jit(solution)/shard_map/ppermute | solution.py:56
  155.9 39.2 %collective-permute-start.42 = (bf16[128,2048]{1,0:T(8,128)(2,1)}, bf16[128,2048]{1,0:T(8,128)(2,1)}, u32[]{:S(2)}, u32[]{:S(2)}) collective-permute-start(bf16[128,2048]{1,0:T(8,128)(2,1)} %convolution_convert_fusion.21), channel_id=1, source_target_pairs={{0,1},{1,0},{2,3},{3,2},{4,5},{5,4},{6,7},{7,6},{8,9},{9,8},{10,11... | collective-permute-start | bytes 1572872 | tf_op jit(solution)/shard_map/ppermute | solution.py:59
  163.9 133.5 %collective-permute-start.22 = (bf16[128,2048]{1,0:T(8,128)(2,1)}, bf16[128,2048]{1,0:T(8,128)(2,1)}, u32[]{:S(2)}, u32[]{:S(2)}) collective-permute-start(bf16[128,2048]{1,0:T(8,128)(2,1)} %convolution_convert_fusion.27), channel_id=1, source_target_pairs={{0,1},{1,0},{2,3},{3,2},{4,5},{5,4},{6,7},{7,6},{8,9},{9,8},{10,11... | collective-permute-start | bytes 1572872 | tf_op jit(solution)/shard_map/ppermute | solution.py:59
  168.3 24.5 %collective-permute-start.45 = (bf16[128,2048]{1,0:T(8,128)(2,1)}, bf16[128,2048]{1,0:T(8,128)(2,1)}, u32[]{:S(2)}, u32[]{:S(2)}) collective-permute-start(bf16[128,2048]{1,0:T(8,128)(2,1)} %add_convert_fusion.13), channel_id=1, source_target_pairs={{0,4},{1,5},{4,8},{5,9},{8,12},{9,13},{12,14},{13,15},{14,10},{15,... | collective-permute-start | bytes 1572872 | tf_op jit(solution)/shard_map/ppermute | solution.py:53
  168.6 26.6 %collective-permute-start.43 = (bf16[128,2048]{1,0:T(8,128)(2,1)}, bf16[128,2048]{1,0:T(8,128)(2,1)S(1)}, u32[]{:S(2)}, u32[]{:S(2)}) collective-permute-start(bf16[128,2048]{1,0:T(8,128)(2,1)} %add_convert_fusion.14), channel_id=1, source_target_pairs={{0,2},{1,3},{4,0},{5,1},{8,4},{9,5},{12,8},{13,9},{14,12},{15,13},... | collective-permute-start | bytes 1572872 | tf_op jit(solution)/shard_map/ppermute | solution.py:56
  211.4 24.0 %collective-permute-start.52 = (bf16[128,2048]{1,0:T(8,128)(2,1)}, bf16[128,2048]{1,0:T(8,128)(2,1)}, u32[]{:S(2)}, u32[]{:S(2)}) collective-permute-start(bf16[128,2048]{1,0:T(8,128)(2,1)} %convolution_convert_fusion.15), channel_id=1, source_target_pairs={{0,1},{1,0},{2,3},{3,2},{4,5},{5,4},{6,7},{7,6},{8,9},{9,8},{10,11... | collective-permute-start | bytes 1572872 | tf_op jit(solution)/shard_map/ppermute | solution.py:59
  212.5 46.1 %collective-permute-start.51 = (bf16[128,2048]{1,0:T(8,128)(2,1)}, bf16[128,2048]{1,0:T(8,128)(2,1)}, u32[]{:S(2)}, u32[]{:S(2)}) collective-permute-start(bf16[128,2048]{1,0:T(8,128)(2,1)} %convolution_convert_fusion.16), channel_id=1, source_target_pairs={{0,1},{1,0},{2,3},{3,2},{4,5},{5,4},{6,7},{7,6},{8,9},{9,8},{10,11... | collective-permute-start | bytes 1572872 | tf_op jit(solution)/shard_map/ppermute | solution.py:59
  224.1 45.0 %collective-permute-start.50 = (bf16[128,2048]{1,0:T(8,128)(2,1)}, bf16[128,2048]{1,0:T(8,128)(2,1)}, u32[]{:S(2)}, u32[]{:S(2)}) collective-permute-start(bf16[128,2048]{1,0:T(8,128)(2,1)} %convolution_convert_fusion.17), channel_id=1, source_target_pairs={{0,1},{1,0},{2,3},{3,2},{4,5},{5,4},{6,7},{7,6},{8,9},{9,8},{10,11... | collective-permute-start | bytes 1572872 | tf_op jit(solution)/shard_map/ppermute | solution.py:59
  230.6 31.9 %collective-permute-start.59 = (bf16[128,2048]{1,0:T(8,128)(2,1)}, bf16[128,2048]{1,0:T(8,128)(2,1)}, u32[]{:S(2)}, u32[]{:S(2)}) collective-permute-start(bf16[128,2048]{1,0:T(8,128)(2,1)} %convolution_convert_fusion.12), channel_id=1, source_target_pairs={{0,1},{1,0},{2,3},{3,2},{4,5},{5,4},{6,7},{7,6},{8,9},{9,8},{10,11... | collective-permute-start | bytes 1572872 | tf_op jit(solution)/shard_map/ppermute | solution.py:59
  236.9 21.9 %collective-permute-start.53 = (bf16[64,2048]{1,0:T(8,128)(2,1)S(1)}, bf16[64,2048]{1,0:T(8,128)(2,1)S(1)}, u32[]{:S(2)}, u32[]{:S(2)}) collective-permute-start(bf16[64,2048]{1,0:T(8,128)(2,1)S(1)} %get-tuple-element.72), channel_id=1, source_target_pairs={{0,2},{1,3},{4,0},{5,1},{8,4},{9,5},{12,8},{13,9},{14,12},{15,13},... | collective-permute-start | bytes 786440 | tf_op jit(solution)/shard_map/ppermute | solution.py:56
  258.7 8.6 %collective-permute-start.60 = (bf16[64,2048]{1,0:T(8,128)(2,1)S(1)}, bf16[64,2048]{1,0:T(8,128)(2,1)S(1)}, u32[]{:S(2)}, u32[]{:S(2)}) collective-permute-start(bf16[64,2048]{1,0:T(8,128)(2,1)S(1)} %get-tuple-element.73), channel_id=1, source_target_pairs={{0,4},{1,5},{4,8},{5,9},{8,12},{9,13},{12,14},{13,15},{14,10},{15,... | collective-permute-start | bytes 786440 | tf_op jit(solution)/shard_map/ppermute | solution.py:53
  260.2 14.2 %collective-permute-start.54 = (bf16[128,2048]{1,0:T(8,128)(2,1)S(1)}, bf16[128,2048]{1,0:T(8,128)(2,1)S(1)}, u32[]{:S(2)}, u32[]{:S(2)}) collective-permute-start(bf16[128,2048]{1,0:T(8,128)(2,1)S(1)} %add_convert_fusion.8), channel_id=1, source_target_pairs={{0,2},{1,3},{4,0},{5,1},{8,4},{9,5},{12,8},{13,9},{14,12},{15,13},... | collective-permute-start | bytes 1572872 | tf_op jit(solution)/shard_map/ppermute | solution.py:56
  262.6 13.1 %collective-permute-start.58 = (bf16[128,2048]{1,0:T(8,128)(2,1)S(1)}, bf16[128,2048]{1,0:T(8,128)(2,1)S(1)}, u32[]{:S(2)}, u32[]{:S(2)}) collective-permute-start(bf16[128,2048]{1,0:T(8,128)(2,1)S(1)} %copy-done.19), channel_id=1, source_target_pairs={{0,1},{1,0},{2,3},{3,2},{4,5},{5,4},{6,7},{7,6},{8,9},{9,8},{10,11... | collective-permute-start | bytes 1572872 | tf_op jit(solution)/shard_map/ppermute | solution.py:59
  268.7 13.4 %collective-permute-start.61 = (bf16[128,2048]{1,0:T(8,128)(2,1)S(1)}, bf16[128,2048]{1,0:T(8,128)(2,1)S(1)}, u32[]{:S(2)}, u32[]{:S(2)}) collective-permute-start(bf16[128,2048]{1,0:T(8,128)(2,1)S(1)} %add_convert_fusion.5), channel_id=1, source_target_pairs={{0,4},{1,5},{4,8},{5,9},{8,12},{9,13},{12,14},{13,15},{14,10},{15,... | collective-permute-start | bytes 1572872 | tf_op jit(solution)/shard_map/ppermute | solution.py:53
  269.1 14.4 %collective-permute-start.49 = (bf16[128,2048]{1,0:T(8,128)(2,1)S(1)}, bf16[128,2048]{1,0:T(8,128)(2,1)S(1)}, u32[]{:S(2)}, u32[]{:S(2)}) collective-permute-start(bf16[128,2048]{1,0:T(8,128)(2,1)S(1)} %copy-done.18), channel_id=1, source_target_pairs={{0,1},{1,0},{2,3},{3,2},{4,5},{5,4},{6,7},{7,6},{8,9},{9,8},{10,11... | collective-permute-start | bytes 1572872 | tf_op jit(solution)/shard_map/ppermute | solution.py:59
  274.4 16.3 %collective-permute-start.57 = (bf16[128,2048]{1,0:T(8,128)(2,1)S(1)}, bf16[128,2048]{1,0:T(8,128)(2,1)S(1)}, u32[]{:S(2)}, u32[]{:S(2)}) collective-permute-start(bf16[128,2048]{1,0:T(8,128)(2,1)S(1)} %convolution_convert_fusion.14), channel_id=1, source_target_pairs={{0,1},{1,0},{2,3},{3,2},{4,5},{5,4},{6,7},{7,6},{8,9},{9,8},{10,11... | collective-permute-start | bytes 1572872 | tf_op jit(solution)/shard_map/ppermute | solution.py:59
  275.6 14.8 %collective-permute-start.55 = (bf16[128,2048]{1,0:T(8,128)(2,1)S(1)}, bf16[128,2048]{1,0:T(8,128)(2,1)S(1)}, u32[]{:S(2)}, u32[]{:S(2)}) collective-permute-start(bf16[128,2048]{1,0:T(8,128)(2,1)S(1)} %add_convert_fusion.7), channel_id=1, source_target_pairs={{0,2},{1,3},{4,0},{5,1},{8,4},{9,5},{12,8},{13,9},{14,12},{15,13},... | collective-permute-start | bytes 1572872 | tf_op jit(solution)/shard_map/ppermute | solution.py:56
  282.3 14.9 %collective-permute-start.62 = (bf16[128,2048]{1,0:T(8,128)(2,1)S(1)}, bf16[128,2048]{1,0:T(8,128)(2,1)S(1)}, u32[]{:S(2)}, u32[]{:S(2)}) collective-permute-start(bf16[128,2048]{1,0:T(8,128)(2,1)S(1)} %add_convert_fusion.4), channel_id=1, source_target_pairs={{0,4},{1,5},{4,8},{5,9},{8,12},{9,13},{12,14},{13,15},{14,10},{15,... | collective-permute-start | bytes 1572872 | tf_op jit(solution)/shard_map/ppermute | solution.py:53
  283.5 18.1 %collective-permute-start.46 = (bf16[128,2048]{1,0:T(8,128)(2,1)S(1)}, bf16[128,2048]{1,0:T(8,128)(2,1)S(1)}, u32[]{:S(2)}, u32[]{:S(2)}) collective-permute-start(bf16[128,2048]{1,0:T(8,128)(2,1)S(1)} %copy-done.16), channel_id=1, source_target_pairs={{0,2},{1,3},{4,0},{5,1},{8,4},{9,5},{12,8},{13,9},{14,12},{15,13},... | collective-permute-start | bytes 1572872 | tf_op jit(solution)/shard_map/ppermute | solution.py:56
  290.4 18.1 %collective-permute-start.47 = (bf16[128,2048]{1,0:T(8,128)(2,1)S(1)}, bf16[128,2048]{1,0:T(8,128)(2,1)S(1)}, u32[]{:S(2)}, u32[]{:S(2)}) collective-permute-start(bf16[128,2048]{1,0:T(8,128)(2,1)S(1)} %copy-done.15), channel_id=1, source_target_pairs={{0,4},{1,5},{4,8},{5,9},{8,12},{9,13},{12,14},{13,15},{14,10},{15,... | collective-permute-start | bytes 1572872 | tf_op jit(solution)/shard_map/ppermute | solution.py:53
  290.6 20.0 %collective-permute-start.48 = (bf16[128,2048]{1,0:T(8,128)(2,1)S(1)}, bf16[128,2048]{1,0:T(8,128)(2,1)S(1)}, u32[]{:S(2)}, u32[]{:S(2)}) collective-permute-start(bf16[128,2048]{1,0:T(8,128)(2,1)S(1)} %convolution_convert_fusion.19), channel_id=1, source_target_pairs={{0,1},{1,0},{2,3},{3,2},{4,5},{5,4},{6,7},{7,6},{8,9},{9,8},{10,11... | collective-permute-start | bytes 1572872 | tf_op jit(solution)/shard_map/ppermute | solution.py:59
  297.2 15.3 %collective-permute-start.56 = (bf16[128,2048]{1,0:T(8,128)(2,1)S(1)}, bf16[128,2048]{1,0:T(8,128)(2,1)S(1)}, u32[]{:S(2)}, u32[]{:S(2)}) collective-permute-start(bf16[128,2048]{1,0:T(8,128)(2,1)S(1)} %add_convert_fusion.6), channel_id=1, source_target_pairs={{0,2},{1,3},{4,0},{5,1},{8,4},{9,5},{12,8},{13,9},{14,12},{15,13},... | collective-permute-start | bytes 1572872 | tf_op jit(solution)/shard_map/ppermute | solution.py:56
  297.5 19.8 %collective-permute-start.63 = (bf16[128,2048]{1,0:T(8,128)(2,1)S(1)}, bf16[128,2048]{1,0:T(8,128)(2,1)S(1)}, u32[]{:S(2)}, u32[]{:S(2)}) collective-permute-start(bf16[128,2048]{1,0:T(8,128)(2,1)S(1)} %add_convert_fusion.3), channel_id=1, source_target_pairs={{0,4},{1,5},{4,8},{5,9},{8,12},{9,13},{12,14},{13,15},{14,10},{15,... | collective-permute-start | bytes 1572872 | tf_op jit(solution)/shard_map/ppermute | solution.py:53
  (70 other events, 2112.8 us)
